TPU v7x, 32 devices: a whole 2x2x4 slice. The times are simulated.
32 devices in a mesh: req: 16 (over z, x, core), head: 2 (over y).
Axes of the slice: x: 2, y: 2, z: 4, core: 2. Of those that a mesh axis runs over, the one named last changes fastest.
Arguments:
- queries: bfloat16 [32, 256, 64, 128], P('req', None, 'head'), may hold values from -9 to 9
- fresh_key_value: bfloat16 [2, 32, 256, 8, 128], P(None, 'req', None, 'head'), may hold values from -6 to 6
- prefix_kv: bfloat16 [2, 32, 8, 128, 128], P(None, 'req', 'head'), may hold values from -6 to 6
- block_mask: int32 [32, 32], P('req'), may hold values from 0 to 1, as said below
- valid_tokens: int32 [32], replicated, may hold values from 1 to 128, as said below
Outputs:
- context: bfloat16 [8192, 8192], P(('req', 'head'))
Inputs may be any that keep to these rules, and one draw needn't show every extreme that they name: `block_mask`: row r marks the blocks on the path from block 0 down to one block of a prefix tree in which every block's parent has a lower index; a path holds at most 6 blocks, and row 0 holds exactly 6. A path holds at most one block of each aligned group of 2 blocks; block 1 is read by no request. The requests of one index of req read at most 2 blocks of one aligned group, and those of index 0 read exactly 2 blocks of group 1. `valid_tokens`: A block that is the parent of some block holds 128 tokens; block 0 is such a block.
All inputs are finite; a program needn't handle non-finite values.
Results may differ from a plain program's by a relative error of at most 0.006.
Values may be sent and summed in bfloat16 or wider, within the bound.
A program may use at most 128 MiB of HBM per device.

v0:
```python
import jax
import jax.numpy as jnp
from jax import lax
from jax.sharding import PartitionSpec as P

masked_score = -1e30


def block_update(carried, grouped_heads, key_rows, value_rows, allowed, score_scale):
    maxima, totals, accumulated = carried
    scores = (
        jnp.einsum("rtkgd,kjd->rtkgj", grouped_heads, key_rows, preferred_element_type=jnp.float32)
        * score_scale
    )
    allowed_wide = allowed[:, None, None, None, :]
    scores = jnp.where(allowed_wide, scores, masked_score)
    newmax = jnp.maximum(maxima, jnp.max(scores, axis=-1))
    factor = jnp.exp(maxima - newmax)
    weights = jnp.where(allowed_wide, jnp.exp(scores - newmax[..., None]), 0.0)
    totals = totals * factor + jnp.sum(weights, axis=-1)
    product = jnp.einsum(
        "rtkgj,kjd->rtkgd",
        weights.astype(jnp.bfloat16),
        value_rows,
        preferred_element_type=jnp.float32,
    )
    accumulated = accumulated * factor[..., None] + product
    return (newmax, totals, accumulated)


def own_state(grouped_heads, fresh_key_value, score_scale):
    scores = (
        jnp.einsum(
            "rtkgd,rskd->rtkgs",
            grouped_heads,
            fresh_key_value[0],
            preferred_element_type=jnp.float32,
        )
        * score_scale
    )
    length = scores.shape[1]
    causal = jnp.arange(length)[:, None] >= jnp.arange(length)[None, :]
    allowed_wide = causal[None, :, None, None, :]
    scores = jnp.where(allowed_wide, scores, masked_score)
    maxima = jnp.max(scores, axis=-1)
    weights = jnp.where(allowed_wide, jnp.exp(scores - maxima[..., None]), 0.0)
    totals = jnp.sum(weights, axis=-1)
    accumulated = jnp.einsum(
        "rtkgs,rskd->rtkgd",
        weights.astype(jnp.bfloat16),
        fresh_key_value[1],
        preferred_element_type=jnp.float32,
    )
    return (maxima, totals, accumulated)


def fold_piece(carried, shard_kv, first_block, block_step):

    def one_block(position, inner):
        return block_step(
            inner,
            shard_kv[0][position],
            shard_kv[1][position],
            first_block + position,
            jnp.asarray(True),
        )

    return lax.fori_loop(0, shard_kv.shape[1], one_block, carried)


def per_device(queries, fresh_key_value, prefix_kv, block_mask, valid_tokens):
    requests, length, local_heads, head_size = queries.shape
    local_kv = fresh_key_value.shape[3]
    grouped_heads = queries.reshape(requests, length, local_kv, local_heads // local_kv, head_size)
    score_scale = head_size ** (-0.5)
    slot_range = jnp.arange(prefix_kv.shape[3])

    def plain_step(inner, key_rows, value_rows, block_index, present):
        block_index = jnp.asarray(block_index, jnp.int32)
        row_reads = lax.dynamic_index_in_dim(block_mask, block_index, 1, keepdims=False)
        block_limit = lax.dynamic_index_in_dim(valid_tokens, block_index, 0, keepdims=False)
        allowed = (row_reads[:, None] == 1) & (slot_range[None, :] < block_limit) & present
        return block_update(inner, grouped_heads, key_rows, value_rows, allowed, score_scale)

    def block_step(inner, key_rows, value_rows, block_index, present):
        block_index = jnp.asarray(block_index, jnp.int32)
        row_reads = lax.dynamic_index_in_dim(block_mask, block_index, 1, keepdims=False)
        return lax.cond(
            jnp.any(row_reads == 1) & present,
            lambda kept: plain_step(kept, key_rows, value_rows, block_index, present),
            lambda kept: kept,
            inner,
        )

    carried = own_state(grouped_heads, fresh_key_value, score_scale)
    carried = fold_piece(
        carried, lax.all_gather(prefix_kv, "req", axis=1, tiled=True), jnp.int32(0), block_step
    )
    maxima, totals, accumulated = carried
    context = (accumulated / totals[..., None]).astype(jnp.bfloat16)
    context = context.reshape(requests * length, local_heads * head_size)
    return lax.all_to_all(context, "head", split_axis=0, concat_axis=1, tiled=True)


def solution(mesh):
    return jax.shard_map(
        per_device,
        mesh=mesh,
        in_specs=(
            P("req", None, "head", None),
            P(None, "req", None, "head", None),
            P(None, "req", "head", None, None),
            P("req", None),
            P(),
        ),
        out_specs=P(("req", "head"), None),
        check_vma=False,
    )
```

profile of v0, /device:TPU:0, one launch (start us, length us, event | category | flops | bytes accessed | tf_op | source)
XLA Modules:
  0.0 342.0 jit_solution(7411989051648773025)
XLA Ops:
  7.3 6.0 %copy.35 = bf16[2,256,4,8,128]{4,1,3,0,2:T(8,128)(2,1)} copy(bf16[2,256,4,8,128]{4,3,2,1,0:T(8,128)(2,1)} %bitcast.73) | data formatting | bytes 8388608
  13.7 8.1 %fusion.24 = (f32[2,256,4,8]{1,3,2,0:T(8,128)S(1)}, f32[2,4,256,256,8]{3,2,4,1,0:T(8,128)}) fusion(pred[256,256]{0,1:T(8,128)(4,1)S(1)} %iota_compare_fusion, bf16[2,256,4,8,128]{4,3,2,1,0:T(8,128)(2,1)S(1)} %bitcast.74, bf16[1,2,256,4,128]{4,3,2,1,0:T(4,128)(2,1)S(1)} %get-tuple-element.331), kind=kOutput, calls=%fused_computation.32 | convolution fusion | flops 1086308352 | bytes 21626880 | tf_op jit(solution)/shard_map/rtkgd,rskd->rtkgs/dot_general | solution.py:33
  21.8 14.0 %fusion.36 = f32[2,256,4,8,128]{4,1,3,2,0:T(8,128)} fusion(f32[2,4,256,256,8]{3,2,4,1,0:T(8,128)} %get-tuple-element.333, f32[2,256,4,8]{1,3,2,0:T(8,128)S(1)} %get-tuple-element.332, pred[256,256]{0,1:T(8,128)(4,1)S(1)} %iota_compare_fusion, bf16[1,2,256,4,128]{4,3,2,1,0:T(4,128)(2,1)S(1)} %get-tuple-element.330), kind=kOutput, calls=%fused_computation.44 | convolution fusion | flops 1094713344 | bytes 25821184 | tf_op jit(solution)/shard_map/rtkgs,rskd->rtkgd/dot_general | solution.py:48
  35.7 8.8 %copy.33 = f32[2,256,4,8,128]{4,1,3,0,2:T(8,128)} copy(f32[2,256,4,8,128]{4,1,3,2,0:T(8,128)} %fusion.36) | data formatting | bytes 16777216
  47.7 4.2 %fusion.26 = f32[2,256,4,8]{1,3,2,0:T(8,128)S(1)} fusion(f32[2,4,256,256,8]{3,2,4,1,0:T(8,128)S(1)} %copy-done.2, f32[2,256,4,8]{1,3,2,0:T(8,128)S(1)} %get-tuple-element.332, pred[256,256]{0,1:T(8,128)(4,1)S(1)} %iota_compare_fusion), kind=kLoop, calls=%fused_computation.34 | loop fusion | flops 20955136 | bytes 16973824 | tf_op jit(solution)/shard_map/reduce_sum | solution.py:47
  52.0 35.2 %all-gather.2.cloned.1.call-done = bf16[2,32,4,128,128]{4,3,2,1,0:T(8,128)(2,1)} async-done(((bf16[2,2,4,128,128]{4,3,2,1,0:T(8,128)(2,1)}), bf16[2,32,4,128,128]{4,3,2,1,0:T(8,128)(2,1)}) %all-gather.2.cloned.1.call-update) | async-done | bytes 8388624 | tf_op jit(solution)/shard_map/all_gather | solution.py:97
  87.2 176.5 %while.18 = (s32[]{:T(128)}, f32[2,256,4,8]{1,3,0,2:T(8,128)S(1)}, f32[2,256,4,8]{1,3,0,2:T(8,128)S(1)}, f32[2,256,4,8,128]{4,1,3,0,2:T(8,128)}, s32[2,32]{0,1:T...) while((s32[]{:T(128)}, f32[2,256,4,8]{1,3,0,2:T(8,128)S(1)}, ...), condition=%wide.region_8.9_spmd.clone, body=%wide.region_2.8_spmd.clone.sunk | while | flops 1105232256 | bytes 139726000 | solution.py:68
  88.5 19.1 %conditional.3 = ((f32[2,256,4,8]{1,3,0,2:T(8,128)S(1)}, f32[2,256,4,8]{1,3,0,2:T(8,128)S(1)}, f32[2,256,4,8,128]{4,1,3,0,2:T(8,128)})) conditional(s32[]{:T(128)} %convert_element_type.31, (f32[2,256,4,8]{1,3,0,2:T(8,128)S(1)}, f32[2,256,4,8]{1,3,0,2:T(8,128)S(1)}, f32[2,256,4,8,128]{4,1,3,0,2:T(8,128)}) %tuple.54, (s32[]{:T(128)}, ...), branch_computations={%region_4.4_spmd, %region_5.7_spmd} | conditional | flops 1105232256 | bytes 139725280 | solution.py:88
  89.9 4.0 %fusion.42 = (bf16[1,32,4,128,128]{4,3,2,1,0:T(8,128)(2,1)S(1)}, bf16[1,32,4,128,128]{4,3,2,1,0:T(8,128)(2,1)S(1)}) fusion(bf16[2,32,4,128,128]{4,3,2,1,0:T(8,128)(2,1)} %get-tuple-element.242), kind=kLoop, calls=%fused_computation.51 | loop fusion | bytes 16777216 | tf_op jit(solution)/shard_map/while/body/eval_jaxpr/slice | solution.py:63
  98.4 5.9 %bitcast_add_fusion = f32[2,256,4,8,128]{4,1,3,0,2:T(8,128)S(1)} fusion(f32[2,256,4,8,128]{4,1,3,0,2:T(8,128)S(1)} %bitcast.70, f32[2,256,4,8]{1,3,0,2:T(8,128)S(1)} %get-tuple-element.325, f32[4,128,2,256,8]{3,1,4,2,0:T(8,128)S(1)} %get-tuple-element.329, f32[2,256,4,8]{1,3,0,2:T(8,128)S(1)} %max.4, pred[2,128]{1,0:T(4,128)(4,1)S(1)} %broadcast_and_fusion, ...), kind=kOutput, calls=%fused_computation.1 | convolution fusion | flops 551550976 | bytes 25428484 | tf_op jit(solution)/shard_map/while/body/eval_jaxpr/cond/branch_1_fun/rtkgj,kjd->rtkgd/dot_general | solution.py:21
  110.2 19.1 %conditional.3 = ((f32[2,256,4,8]{1,3,0,2:T(8,128)S(1)}, f32[2,256,4,8]{1,3,0,2:T(8,128)S(1)}, f32[2,256,4,8,128]{4,1,3,0,2:T(8,128)})) conditional(s32[]{:T(128)} %convert_element_type.31, (f32[2,256,4,8]{1,3,0,2:T(8,128)S(1)}, f32[2,256,4,8]{1,3,0,2:T(8,128)S(1)}, f32[2,256,4,8,128]{4,1,3,0,2:T(8,128)}) %tuple.54, (s32[]{:T(128)}, ...), branch_computations={%region_4.4_spmd, %region_5.7_spmd} | conditional | flops 1105232256 | bytes 139725280 | solution.py:88
  111.6 4.0 %fusion.42 = (bf16[1,32,4,128,128]{4,3,2,1,0:T(8,128)(2,1)S(1)}, bf16[1,32,4,128,128]{4,3,2,1,0:T(8,128)(2,1)S(1)}) fusion(bf16[2,32,4,128,128]{4,3,2,1,0:T(8,128)(2,1)} %get-tuple-element.242), kind=kLoop, calls=%fused_computation.51 | loop fusion | bytes 16777216 | tf_op jit(solution)/shard_map/while/body/eval_jaxpr/slice | solution.py:63
  120.2 5.9 %bitcast_add_fusion = f32[2,256,4,8,128]{4,1,3,0,2:T(8,128)S(1)} fusion(f32[2,256,4,8,128]{4,1,3,0,2:T(8,128)S(1)} %bitcast.70, f32[2,256,4,8]{1,3,0,2:T(8,128)S(1)} %get-tuple-element.325, f32[4,128,2,256,8]{3,1,4,2,0:T(8,128)S(1)} %get-tuple-element.329, f32[2,256,4,8]{1,3,0,2:T(8,128)S(1)} %max.4, pred[2,128]{1,0:T(4,128)(4,1)S(1)} %broadcast_and_fusion, ...), kind=kOutput, calls=%fused_computation.1 | convolution fusion | flops 551550976 | bytes 25428484 | tf_op jit(solution)/shard_map/while/body/eval_jaxpr/cond/branch_1_fun/rtkgj,kjd->rtkgd/dot_general | solution.py:21
  130.6 19.1 %conditional.3 = ((f32[2,256,4,8]{1,3,0,2:T(8,128)S(1)}, f32[2,256,4,8]{1,3,0,2:T(8,128)S(1)}, f32[2,256,4,8,128]{4,1,3,0,2:T(8,128)})) conditional(s32[]{:T(128)} %convert_element_type.31, (f32[2,256,4,8]{1,3,0,2:T(8,128)S(1)}, f32[2,256,4,8]{1,3,0,2:T(8,128)S(1)}, f32[2,256,4,8,128]{4,1,3,0,2:T(8,128)}) %tuple.54, (s32[]{:T(128)}, ...), branch_computations={%region_4.4_spmd, %region_5.7_spmd} | conditional | flops 1105232256 | bytes 139725280 | solution.py:88
  132.0 4.0 %fusion.42 = (bf16[1,32,4,128,128]{4,3,2,1,0:T(8,128)(2,1)S(1)}, bf16[1,32,4,128,128]{4,3,2,1,0:T(8,128)(2,1)S(1)}) fusion(bf16[2,32,4,128,128]{4,3,2,1,0:T(8,128)(2,1)} %get-tuple-element.242), kind=kLoop, calls=%fused_computation.51 | loop fusion | bytes 16777216 | tf_op jit(solution)/shard_map/while/body/eval_jaxpr/slice | solution.py:63
  140.5 5.9 %bitcast_add_fusion = f32[2,256,4,8,128]{4,1,3,0,2:T(8,128)S(1)} fusion(f32[2,256,4,8,128]{4,1,3,0,2:T(8,128)S(1)} %bitcast.70, f32[2,256,4,8]{1,3,0,2:T(8,128)S(1)} %get-tuple-element.325, f32[4,128,2,256,8]{3,1,4,2,0:T(8,128)S(1)} %get-tuple-element.329, f32[2,256,4,8]{1,3,0,2:T(8,128)S(1)} %max.4, pred[2,128]{1,0:T(4,128)(4,1)S(1)} %broadcast_and_fusion, ...), kind=kOutput, calls=%fused_computation.1 | convolution fusion | flops 551550976 | bytes 25428484 | tf_op jit(solution)/shard_map/while/body/eval_jaxpr/cond/branch_1_fun/rtkgj,kjd->rtkgd/dot_general | solution.py:21
  151.0 19.1 %conditional.3 = ((f32[2,256,4,8]{1,3,0,2:T(8,128)S(1)}, f32[2,256,4,8]{1,3,0,2:T(8,128)S(1)}, f32[2,256,4,8,128]{4,1,3,0,2:T(8,128)})) conditional(s32[]{:T(128)} %convert_element_type.31, (f32[2,256,4,8]{1,3,0,2:T(8,128)S(1)}, f32[2,256,4,8]{1,3,0,2:T(8,128)S(1)}, f32[2,256,4,8,128]{4,1,3,0,2:T(8,128)}) %tuple.54, (s32[]{:T(128)}, ...), branch_computations={%region_4.4_spmd, %region_5.7_spmd} | conditional | flops 1105232256 | bytes 139725280 | solution.py:88
  152.4 4.0 %fusion.42 = (bf16[1,32,4,128,128]{4,3,2,1,0:T(8,128)(2,1)S(1)}, bf16[1,32,4,128,128]{4,3,2,1,0:T(8,128)(2,1)S(1)}) fusion(bf16[2,32,4,128,128]{4,3,2,1,0:T(8,128)(2,1)} %get-tuple-element.242), kind=kLoop, calls=%fused_computation.51 | loop fusion | bytes 16777216 | tf_op jit(solution)/shard_map/while/body/eval_jaxpr/slice | solution.py:63
  160.9 5.9 %bitcast_add_fusion = f32[2,256,4,8,128]{4,1,3,0,2:T(8,128)S(1)} fusion(f32[2,256,4,8,128]{4,1,3,0,2:T(8,128)S(1)} %bitcast.70, f32[2,256,4,8]{1,3,0,2:T(8,128)S(1)} %get-tuple-element.325, f32[4,128,2,256,8]{3,1,4,2,0:T(8,128)S(1)} %get-tuple-element.329, f32[2,256,4,8]{1,3,0,2:T(8,128)S(1)} %max.4, pred[2,128]{1,0:T(4,128)(4,1)S(1)} %broadcast_and_fusion, ...), kind=kOutput, calls=%fused_computation.1 | convolution fusion | flops 551550976 | bytes 25428484 | tf_op jit(solution)/shard_map/while/body/eval_jaxpr/cond/branch_1_fun/rtkgj,kjd->rtkgd/dot_general | solution.py:21
  172.7 19.1 %conditional.3 = ((f32[2,256,4,8]{1,3,0,2:T(8,128)S(1)}, f32[2,256,4,8]{1,3,0,2:T(8,128)S(1)}, f32[2,256,4,8,128]{4,1,3,0,2:T(8,128)})) conditional(s32[]{:T(128)} %convert_element_type.31, (f32[2,256,4,8]{1,3,0,2:T(8,128)S(1)}, f32[2,256,4,8]{1,3,0,2:T(8,128)S(1)}, f32[2,256,4,8,128]{4,1,3,0,2:T(8,128)}) %tuple.54, (s32[]{:T(128)}, ...), branch_computations={%region_4.4_spmd, %region_5.7_spmd} | conditional | flops 1105232256 | bytes 139725280 | solution.py:88
  174.1 4.0 %fusion.42 = (bf16[1,32,4,128,128]{4,3,2,1,0:T(8,128)(2,1)S(1)}, bf16[1,32,4,128,128]{4,3,2,1,0:T(8,128)(2,1)S(1)}) fusion(bf16[2,32,4,128,128]{4,3,2,1,0:T(8,128)(2,1)} %get-tuple-element.242), kind=kLoop, calls=%fused_computation.51 | loop fusion | bytes 16777216 | tf_op jit(solution)/shard_map/while/body/eval_jaxpr/slice | solution.py:63
  182.6 5.9 %bitcast_add_fusion = f32[2,256,4,8,128]{4,1,3,0,2:T(8,128)S(1)} fusion(f32[2,256,4,8,128]{4,1,3,0,2:T(8,128)S(1)} %bitcast.70, f32[2,256,4,8]{1,3,0,2:T(8,128)S(1)} %get-tuple-element.325, f32[4,128,2,256,8]{3,1,4,2,0:T(8,128)S(1)} %get-tuple-element.329, f32[2,256,4,8]{1,3,0,2:T(8,128)S(1)} %max.4, pred[2,128]{1,0:T(4,128)(4,1)S(1)} %broadcast_and_fusion, ...), kind=kOutput, calls=%fused_computation.1 | convolution fusion | flops 551550976 | bytes 25428484 | tf_op jit(solution)/shard_map/while/body/eval_jaxpr/cond/branch_1_fun/rtkgj,kjd->rtkgd/dot_general | solution.py:21
  194.5 19.1 %conditional.3 = ((f32[2,256,4,8]{1,3,0,2:T(8,128)S(1)}, f32[2,256,4,8]{1,3,0,2:T(8,128)S(1)}, f32[2,256,4,8,128]{4,1,3,0,2:T(8,128)})) conditional(s32[]{:T(128)} %convert_element_type.31, (f32[2,256,4,8]{1,3,0,2:T(8,128)S(1)}, f32[2,256,4,8]{1,3,0,2:T(8,128)S(1)}, f32[2,256,4,8,128]{4,1,3,0,2:T(8,128)}) %tuple.54, (s32[]{:T(128)}, ...), branch_computations={%region_4.4_spmd, %region_5.7_spmd} | conditional | flops 1105232256 | bytes 139725280 | solution.py:88
  195.8 4.0 %fusion.42 = (bf16[1,32,4,128,128]{4,3,2,1,0:T(8,128)(2,1)S(1)}, bf16[1,32,4,128,128]{4,3,2,1,0:T(8,128)(2,1)S(1)}) fusion(bf16[2,32,4,128,128]{4,3,2,1,0:T(8,128)(2,1)} %get-tuple-element.242), kind=kLoop, calls=%fused_computation.51 | loop fusion | bytes 16777216 | tf_op jit(solution)/shard_map/while/body/eval_jaxpr/slice | solution.py:63
  204.4 5.9 %bitcast_add_fusion = f32[2,256,4,8,128]{4,1,3,0,2:T(8,128)S(1)} fusion(f32[2,256,4,8,128]{4,1,3,0,2:T(8,128)S(1)} %bitcast.70, f32[2,256,4,8]{1,3,0,2:T(8,128)S(1)} %get-tuple-element.325, f32[4,128,2,256,8]{3,1,4,2,0:T(8,128)S(1)} %get-tuple-element.329, f32[2,256,4,8]{1,3,0,2:T(8,128)S(1)} %max.4, pred[2,128]{1,0:T(4,128)(4,1)S(1)} %broadcast_and_fusion, ...), kind=kOutput, calls=%fused_computation.1 | convolution fusion | flops 551550976 | bytes 25428484 | tf_op jit(solution)/shard_map/while/body/eval_jaxpr/cond/branch_1_fun/rtkgj,kjd->rtkgd/dot_general | solution.py:21
  216.2 19.1 %conditional.3 = ((f32[2,256,4,8]{1,3,0,2:T(8,128)S(1)}, f32[2,256,4,8]{1,3,0,2:T(8,128)S(1)}, f32[2,256,4,8,128]{4,1,3,0,2:T(8,128)})) conditional(s32[]{:T(128)} %convert_element_type.31, (f32[2,256,4,8]{1,3,0,2:T(8,128)S(1)}, f32[2,256,4,8]{1,3,0,2:T(8,128)S(1)}, f32[2,256,4,8,128]{4,1,3,0,2:T(8,128)}) %tuple.54, (s32[]{:T(128)}, ...), branch_computations={%region_4.4_spmd, %region_5.7_spmd} | conditional | flops 1105232256 | bytes 139725280 | solution.py:88
  217.6 4.0 %fusion.42 = (bf16[1,32,4,128,128]{4,3,2,1,0:T(8,128)(2,1)S(1)}, bf16[1,32,4,128,128]{4,3,2,1,0:T(8,128)(2,1)S(1)}) fusion(bf16[2,32,4,128,128]{4,3,2,1,0:T(8,128)(2,1)} %get-tuple-element.242), kind=kLoop, calls=%fused_computation.51 | loop fusion | bytes 16777216 | tf_op jit(solution)/shard_map/while/body/eval_jaxpr/slice | solution.py:63
  226.1 5.9 %bitcast_add_fusion = f32[2,256,4,8,128]{4,1,3,0,2:T(8,128)S(1)} fusion(f32[2,256,4,8,128]{4,1,3,0,2:T(8,128)S(1)} %bitcast.70, f32[2,256,4,8]{1,3,0,2:T(8,128)S(1)} %get-tuple-element.325, f32[4,128,2,256,8]{3,1,4,2,0:T(8,128)S(1)} %get-tuple-element.329, f32[2,256,4,8]{1,3,0,2:T(8,128)S(1)} %max.4, pred[2,128]{1,0:T(4,128)(4,1)S(1)} %broadcast_and_fusion, ...), kind=kOutput, calls=%fused_computation.1 | convolution fusion | flops 551550976 | bytes 25428484 | tf_op jit(solution)/shard_map/while/body/eval_jaxpr/cond/branch_1_fun/rtkgj,kjd->rtkgd/dot_general | solution.py:21
  263.7 8.7 %copy.37 = f32[2,256,4,8,128]{1,4,3,2,0:T(8,128)} copy(f32[2,256,4,8,128]{4,1,3,0,2:T(8,128)} %get-tuple-element.261) | data formatting | bytes 16777216 | tf_op jit(solution)/shard_map/while | solution.py:68
  272.4 4.6 %divide_convert_fusion = bf16[2,256,4,8,128]{1,4,3,2,0:T(8,128)(2,1)S(1)} fusion(f32[2,256,4,8,128]{1,4,3,2,0:T(8,128)} %copy.37, f32[2,256,4,8]{1,3,0,2:T(8,128)S(1)} %get-tuple-element.262), kind=kLoop, calls=%fused_computation.36 | loop fusion | flops 4194304 | bytes 12648448 | tf_op jit(solution)/shard_map/convert_element_type | solution.py:100
  277.0 51.8 %all_to_all.19 = bf16[2,256,4096]{1,2,0:T(8,128)(2,1)} all-to-all(bf16[2,256,4096]{1,2,0:T(8,128)(2,1)S(1)} %bitcast.71), channel_id=1, replica_groups=mesh['req'=16,'head'=2] {'head'}, dimensions={0} | all-to-all | bytes 8388608 | tf_op jit(solution)/shard_map/all_to_all | solution.py:102
  328.8 6.3 %copy.38 = bf16[256,8192]{1,0:T(8,128)(2,1)} copy(bf16[256,8192]{0,1:T(8,128)(2,1)} %bitcast.72) | data formatting | bytes 8388608 | tf_op jit(solution)/shard_map/all_to_all | solution.py:102
  (232 shorter events, 89.3 us)
Async XLA Ops:
  6.5 6.7 %copy-start.4 = (bf16[2,2,256,4,128]{4,3,2,1,0:T(4,128)(2,1)S(1)}, bf16[2,2,256,4,128]{4,3,2,1,0:T(4,128)(2,1)}, u32[]{:S(2)}) copy-start(bf16[2,2,256,4,128]{4,3,2,1,0:T(4,128)(2,1)} %param.10) | copy-start | bytes 3145732
  6.5 80.7 %all-gather.2.cloned.1.call-start = ((), (), s32[]{:S(2)}) async-start(), calls=%async_computation.1 | async-start | bytes 8912896 | tf_op jit(solution)/shard_map/all_gather | solution.py:97
  7.3 6.4 %copy-start.3 = (bf16[2,256,32,128]{3,2,1,0:T(8,128)(2,1)S(1)}, bf16[2,256,32,128]{3,2,1,0:T(8,128)(2,1)}, u32[]{:S(2)}) copy-start(bf16[2,256,32,128]{3,2,1,0:T(8,128)(2,1)} %param.9) | copy-start | bytes 12582916
  35.7 12.0 %copy-start.2 = (f32[2,4,256,256,8]{3,2,4,1,0:T(8,128)S(1)}, f32[2,4,256,256,8]{3,2,4,1,0:T(8,128)}, u32[]{:S(2)}) copy-start(f32[2,4,256,256,8]{3,2,4,1,0:T(8,128)} %get-tuple-element.333) | copy-start | bytes 50331652
  47.7 4.2 %copy-start.5 = (s32[2,32]{1,0:T(2,128)S(1)}, s32[2,32]{1,0:T(2,128)}, u32[]{:S(2)}) copy-start(s32[2,32]{1,0:T(2,128)} %param.12) | copy-start | bytes 772
  47.7 39.5 %copy-start.6 = (s32[32]{0:T(128)S(1)}, s32[32]{0:T(128)}, u32[]{:S(2)}) copy-start(s32[32]{0:T(128)} %param.13) | copy-start | bytes 388
  89.9 4.7 %copy-start.1 = (bf16[2,256,4,8,128]{4,1,3,0,2:T(8,128)(2,1)S(1)}, bf16[2,256,4,8,128]{4,1,3,0,2:T(8,128)(2,1)}, u32[]{:S(2)}) copy-start(bf16[2,256,4,8,128]{4,1,3,0,2:T(8,128)(2,1)} %get-tuple-element.243) | copy-start | bytes 12582916 | tf_op jit(solution)/shard_map/while/body/eval_jaxpr/cond
  93.9 4.5 %slice-start = ((s8[8388608]{0:T(1024)(128)(4,1)}), s8[4194304]{0:T(1024)(128)(4,1)S(1)}, s32[]{:S(2)}) async-start(s8[8388608]{0:T(1024)(128)(4,1)} %bitcast.69), calls=%async_computation.2 | async-start | bytes 8388608 | tf_op jit(solution)/shard_map/while/body/eval_jaxpr/cond
  94.5 3.9 %slice-start.1 = ((s8[8388608]{0:T(1024)(128)(4,1)}), s8[4194304]{0:T(1024)(128)(4,1)S(1)}, s32[]{:S(2)}) async-start(s8[8388608]{0:T(1024)(128)(4,1)} %bitcast.69), calls=%async_computation.3 | async-start | bytes 8388608 | tf_op jit(solution)/shard_map/while/body/eval_jaxpr/cond
  111.6 4.7 %copy-start.1 = (bf16[2,256,4,8,128]{4,1,3,0,2:T(8,128)(2,1)S(1)}, bf16[2,256,4,8,128]{4,1,3,0,2:T(8,128)(2,1)}, u32[]{:S(2)}) copy-start(bf16[2,256,4,8,128]{4,1,3,0,2:T(8,128)(2,1)} %get-tuple-element.243) | copy-start | bytes 12582916 | tf_op jit(solution)/shard_map/while/body/eval_jaxpr/cond
  115.7 4.5 %slice-start = ((s8[8388608]{0:T(1024)(128)(4,1)}), s8[4194304]{0:T(1024)(128)(4,1)S(1)}, s32[]{:S(2)}) async-start(s8[8388608]{0:T(1024)(128)(4,1)} %bitcast.69), calls=%async_computation.2 | async-start | bytes 8388608 | tf_op jit(solution)/shard_map/while/body/eval_jaxpr/cond
  116.3 3.9 %slice-start.1 = ((s8[8388608]{0:T(1024)(128)(4,1)}), s8[4194304]{0:T(1024)(128)(4,1)S(1)}, s32[]{:S(2)}) async-start(s8[8388608]{0:T(1024)(128)(4,1)} %bitcast.69), calls=%async_computation.3 | async-start | bytes 8388608 | tf_op jit(solution)/shard_map/while/body/eval_jaxpr/cond
  126.1 3.2 copy-start
  132.0 4.7 %copy-start.1 = (bf16[2,256,4,8,128]{4,1,3,0,2:T(8,128)(2,1)S(1)}, bf16[2,256,4,8,128]{4,1,3,0,2:T(8,128)(2,1)}, u32[]{:S(2)}) copy-start(bf16[2,256,4,8,128]{4,1,3,0,2:T(8,128)(2,1)} %get-tuple-element.243) | copy-start | bytes 12582916 | tf_op jit(solution)/shard_map/while/body/eval_jaxpr/cond
  136.0 4.5 %slice-start = ((s8[8388608]{0:T(1024)(128)(4,1)}), s8[4194304]{0:T(1024)(128)(4,1)S(1)}, s32[]{:S(2)}) async-start(s8[8388608]{0:T(1024)(128)(4,1)} %bitcast.69), calls=%async_computation.2 | async-start | bytes 8388608 | tf_op jit(solution)/shard_map/while/body/eval_jaxpr/cond
  136.6 3.9 %slice-start.1 = ((s8[8388608]{0:T(1024)(128)(4,1)}), s8[4194304]{0:T(1024)(128)(4,1)S(1)}, s32[]{:S(2)}) async-start(s8[8388608]{0:T(1024)(128)(4,1)} %bitcast.69), calls=%async_computation.3 | async-start | bytes 8388608 | tf_op jit(solution)/shard_map/while/body/eval_jaxpr/cond
  146.4 3.2 copy-start
  152.4 4.7 %copy-start.1 = (bf16[2,256,4,8,128]{4,1,3,0,2:T(8,128)(2,1)S(1)}, bf16[2,256,4,8,128]{4,1,3,0,2:T(8,128)(2,1)}, u32[]{:S(2)}) copy-start(bf16[2,256,4,8,128]{4,1,3,0,2:T(8,128)(2,1)} %get-tuple-element.243) | copy-start | bytes 12582916 | tf_op jit(solution)/shard_map/while/body/eval_jaxpr/cond
  156.4 4.5 %slice-start = ((s8[8388608]{0:T(1024)(128)(4,1)}), s8[4194304]{0:T(1024)(128)(4,1)S(1)}, s32[]{:S(2)}) async-start(s8[8388608]{0:T(1024)(128)(4,1)} %bitcast.69), calls=%async_computation.2 | async-start | bytes 8388608 | tf_op jit(solution)/shard_map/while/body/eval_jaxpr/cond
  157.0 3.9 %slice-start.1 = ((s8[8388608]{0:T(1024)(128)(4,1)}), s8[4194304]{0:T(1024)(128)(4,1)S(1)}, s32[]{:S(2)}) async-start(s8[8388608]{0:T(1024)(128)(4,1)} %bitcast.69), calls=%async_computation.3 | async-start | bytes 8388608 | tf_op jit(solution)/shard_map/while/body/eval_jaxpr/cond
  166.8 3.2 copy-start
  174.1 4.7 %copy-start.1 = (bf16[2,256,4,8,128]{4,1,3,0,2:T(8,128)(2,1)S(1)}, bf16[2,256,4,8,128]{4,1,3,0,2:T(8,128)(2,1)}, u32[]{:S(2)}) copy-start(bf16[2,256,4,8,128]{4,1,3,0,2:T(8,128)(2,1)} %get-tuple-element.243) | copy-start | bytes 12582916 | tf_op jit(solution)/shard_map/while/body/eval_jaxpr/cond
  178.1 4.5 %slice-start = ((s8[8388608]{0:T(1024)(128)(4,1)}), s8[4194304]{0:T(1024)(128)(4,1)S(1)}, s32[]{:S(2)}) async-start(s8[8388608]{0:T(1024)(128)(4,1)} %bitcast.69), calls=%async_computation.2 | async-start | bytes 8388608 | tf_op jit(solution)/shard_map/while/body/eval_jaxpr/cond
  178.7 3.9 %slice-start.1 = ((s8[8388608]{0:T(1024)(128)(4,1)}), s8[4194304]{0:T(1024)(128)(4,1)S(1)}, s32[]{:S(2)}) async-start(s8[8388608]{0:T(1024)(128)(4,1)} %bitcast.69), calls=%async_computation.3 | async-start | bytes 8388608 | tf_op jit(solution)/shard_map/while/body/eval_jaxpr/cond
  188.6 3.2 copy-start
  195.8 4.7 %copy-start.1 = (bf16[2,256,4,8,128]{4,1,3,0,2:T(8,128)(2,1)S(1)}, bf16[2,256,4,8,128]{4,1,3,0,2:T(8,128)(2,1)}, u32[]{:S(2)}) copy-start(bf16[2,256,4,8,128]{4,1,3,0,2:T(8,128)(2,1)} %get-tuple-element.243) | copy-start | bytes 12582916 | tf_op jit(solution)/shard_map/while/body/eval_jaxpr/cond
  199.9 4.5 %slice-start = ((s8[8388608]{0:T(1024)(128)(4,1)}), s8[4194304]{0:T(1024)(128)(4,1)S(1)}, s32[]{:S(2)}) async-start(s8[8388608]{0:T(1024)(128)(4,1)} %bitcast.69), calls=%async_computation.2 | async-start | bytes 8388608 | tf_op jit(solution)/shard_map/while/body/eval_jaxpr/cond
  200.5 3.9 %slice-start.1 = ((s8[8388608]{0:T(1024)(128)(4,1)}), s8[4194304]{0:T(1024)(128)(4,1)S(1)}, s32[]{:S(2)}) async-start(s8[8388608]{0:T(1024)(128)(4,1)} %bitcast.69), calls=%async_computation.3 | async-start | bytes 8388608 | tf_op jit(solution)/shard_map/while/body/eval_jaxpr/cond
  210.3 3.2 copy-start
  217.6 4.7 %copy-start.1 = (bf16[2,256,4,8,128]{4,1,3,0,2:T(8,128)(2,1)S(1)}, bf16[2,256,4,8,128]{4,1,3,0,2:T(8,128)(2,1)}, u32[]{:S(2)}) copy-start(bf16[2,256,4,8,128]{4,1,3,0,2:T(8,128)(2,1)} %get-tuple-element.243) | copy-start | bytes 12582916 | tf_op jit(solution)/shard_map/while/body/eval_jaxpr/cond
  221.6 4.5 %slice-start = ((s8[8388608]{0:T(1024)(128)(4,1)}), s8[4194304]{0:T(1024)(128)(4,1)S(1)}, s32[]{:S(2)}) async-start(s8[8388608]{0:T(1024)(128)(4,1)} %bitcast.69), calls=%async_computation.2 | async-start | bytes 8388608 | tf_op jit(solution)/shard_map/while/body/eval_jaxpr/cond
  222.2 3.9 %slice-start.1 = ((s8[8388608]{0:T(1024)(128)(4,1)}), s8[4194304]{0:T(1024)(128)(4,1)S(1)}, s32[]{:S(2)}) async-start(s8[8388608]{0:T(1024)(128)(4,1)} %bitcast.69), calls=%async_computation.3 | async-start | bytes 8388608 | tf_op jit(solution)/shard_map/while/body/eval_jaxpr/cond
  (2 other events, 6.4 us)
Sparse Core Ops, SparseCore 0:
  9.5 77.6 all-gather.1
where the time goes:
time: 343 us; the launch traced here: 342 us
  local copies, waits for them, and re-layouts  92.8 us (27%)
  matrix products  73.5 us (21%)
  other arithmetic  52 us (15%)
  blocking collectives  51.8 us (15%)
  waiting for transfers between devices  35.9 us (10%)
  loops' own time  22.5 us (7%)
  between operations  13.5 us (4%)
    all_to_all x1, blocking collectives, per_device(): lax.all_to_all(context, 'head', split_axis=0, concat_axis=1, tiled=True)  51.8 us
    dot_general x7, matrix products, block_update(): jnp.einsum('rtkgj,kjd->rtkgd', weights.astype(jnp.bfloat16), value_rows,...  41.3 us
    all_gather x1, waiting for transfers between devices, per_device(): lax.all_gather(prefix_kv, 'req', axis=1, tiled=True)  35.2 us
    slice x7, local copies, waits for them, and re-layouts, one_block(): shard_kv[1][position]  28.2 us
    cond x63, local copies, waits for them, and re-layouts  26.8 us
    reduce_or x32, other arithmetic, block_step(): jnp.any(row_reads == 1) & present  21.4 us
    another operation x1, loops' own time, fold_piece(): return lax.fori_loop(0, shard_kv.shape[1], one_block, carried)  21.3 us
    unnamed x15, local copies, waits for them, and re-layouts  18 us
  transfers between devices with their start and end apart: 1, of which 1 were waited for; matrix products, arithmetic and copies ran while one was open for 12% of the time, Pallas kernels for 0%

commit v1 on v0

v1 whole, which is shorter than its diff:
```python
import functools
import math

import jax
import jax.numpy as jnp
from jax import lax
from jax.experimental import pallas as pl
from jax.experimental.pallas import tpu as pltpu
from jax.sharding import PartitionSpec as P

PATH = 6
MASKED = -1e30


def attend(chosen, limits, q_ref, fk_ref, fv_ref, *rest):
    k_refs, v_refs, out_ref = rest[:PATH], rest[PATH : 2 * PATH], rest[2 * PATH]
    r = pl.program_id(0)
    tokens, width = q_ref.shape[1], fk_ref.shape[-1]
    slots = k_refs[0].shape[-2]
    group = q_ref.shape[2] // width
    scale = math.log2(math.e) / math.sqrt(width)

    row = lax.broadcasted_iota(jnp.int32, (slots, width), 0)
    marks = [jnp.where(row < limits[r, j], 0.0, MASKED).astype(jnp.bfloat16) for j in range(PATH)]
    keys = jnp.concatenate([k[0, 0, 0] for k in k_refs] + [fk_ref[0, 0]], axis=0)
    marks = jnp.concatenate(marks + [jnp.zeros((tokens, width), jnp.bfloat16)], axis=0)
    keys = jnp.concatenate([keys, marks], axis=1)
    values = jnp.concatenate([v[0, 0, 0] for v in v_refs] + [fv_ref[0, 0]], axis=0)
    values = jnp.concatenate([values, jnp.ones_like(values)], axis=1)
    first = (lax.broadcasted_iota(jnp.int32, (tokens, width), 1) == 0).astype(jnp.bfloat16)
    later = lax.broadcasted_iota(jnp.int32, (tokens, tokens), 0) < lax.broadcasted_iota(
        jnp.int32, (tokens, tokens), 1
    )
    past = PATH * slots
    for g in range(group):
        cols = slice(g * width, (g + 1) * width)
        q = jnp.concatenate([q_ref[0, :, cols], first], axis=1)
        scores = lax.dot_general(
            q, keys, (((1,), (1,)), ((), ())), preferred_element_type=jnp.float32
        )
        own = jnp.where(later, MASKED, scores[:, past:])
        scores = jnp.concatenate([scores[:, :past], own], axis=1)
        peak = jnp.max(scores, axis=1, keepdims=True)
        weights = jnp.exp2((scores - peak) * scale).astype(jnp.bfloat16)
        both = jnp.dot(weights, values, preferred_element_type=jnp.float32)
        out_ref[0, :, cols] = (both[:, :width] / both[:, width:]).astype(jnp.bfloat16)


def attention(queries, fresh, prefix, chosen, limits):
    requests, tokens, heads_wide = queries.shape
    local_kv, slots, width = prefix.shape[2:]
    wide = heads_wide // local_kv

    def block_map(kv, j):
        return lambda r, k, chosen, limits: (kv, chosen[r, j], k, 0, 0)

    def fresh_map(kv):
        return lambda r, k, chosen, limits: (kv, r, 0, k)

    q_spec = pl.BlockSpec((1, tokens, wide), lambda r, k, chosen, limits: (r, 0, k))
    return pl.pallas_call(
        attend,
        out_shape=jax.ShapeDtypeStruct(queries.shape, jnp.bfloat16),
        grid_spec=pltpu.PrefetchScalarGridSpec(
            num_scalar_prefetch=2,
            grid=(requests, local_kv),
            in_specs=[q_spec]
            + [pl.BlockSpec((1, 1, tokens, width), fresh_map(kv)) for kv in (0, 1)]
            + [
                pl.BlockSpec((1, 1, 1, slots, width), block_map(kv, j))
                for kv in (0, 1)
                for j in range(PATH)
            ],
            out_specs=q_spec,
        ),
        compiler_params=pltpu.CompilerParams(vmem_limit_bytes=48 << 20),
    )(chosen, limits, queries, fresh, fresh, *([prefix] * (2 * PATH)))


def per_device(queries, fresh_key_value, prefix_kv, block_mask, valid_tokens):
    requests, length, local_heads, head_size = queries.shape
    blocks = block_mask.shape[1]
    gathered = lax.all_gather(prefix_kv, "req", axis=1, tiled=True)
    order = blocks - jnp.arange(blocks, dtype=jnp.int32)
    ranking = jnp.where(block_mask == 1, order, 0)
    chosen, limits = [], []
    for _ in range(PATH):
        best = jnp.max(ranking, axis=1)
        at = jnp.where(best > 0, blocks - best, 0)
        hit = jnp.arange(blocks)[None, :] == at[:, None]
        chosen.append(at)
        limits.append(jnp.where(best > 0, jnp.sum(jnp.where(hit, valid_tokens[None, :], 0), axis=1), 0))
        ranking = jnp.where(hit, 0, ranking)
    chosen = jnp.stack(chosen, axis=1).astype(jnp.int32)
    limits = jnp.stack(limits, axis=1).astype(jnp.int32)
    q = queries.reshape(requests, length, local_heads * head_size)
    fresh = fresh_key_value.reshape(2, requests, length, -1)
    context = attention(q, fresh, gathered, chosen, limits)
    parts = lax.axis_size("head")
    context = context.reshape(parts, requests * length // parts, local_heads * head_size)
    swapped = lax.all_to_all(context, "head", split_axis=0, concat_axis=0)
    return jnp.concatenate([swapped[i] for i in range(parts)], axis=1)


def solution(mesh):
    return jax.shard_map(
        per_device,
        mesh=mesh,
        in_specs=(
            P("req", None, "head", None),
            P(None, "req", None, "head", None),
            P(None, "req", "head", None, None),
            P("req", None),
            P(),
        ),
        out_specs=P(("req", "head"), None),
        check_vma=False,
    )
```

time: 343 us -> 175 us (0.51)
  local copies, waits for them, and re-layouts: 92.8 us -> 10.6 us
  matrix products: 73.5 us -> 0 us
  other arithmetic: 52 us -> 6.53 us
  waiting for transfers between devices: 35.9 us -> 66.4 us
  Pallas kernels: 0 us -> 26.9 us
  loops' own time: 22.5 us -> 0 us
    dot_general x16 -> x0, matrix products: 73.5 us -> none  [the longest x7 41.3 us: block_update(): jnp.einsum('rtkgj,kjd->rtkgd', weights.astype(jnp.bfloat16), value_rows,...]
    all_gather x1, waiting for transfers between devices: 35.2 us -> 65.7 us  [per_device(): gathered = lax.all_gather(prefix_kv, 'req', axis=1, tiled=True)]
    slice x8 -> x0, local copies, waits for them, and re-layouts: 28.6 us -> none  [the longest x7 28.2 us: one_block(): shard_kv[1][position]]
    pallas_call x0 -> x1, Pallas kernels: none -> 26.9 us  [attention(): pl.pallas_call(attend, out_shape=jax.ShapeDtypeStruct(queries.shape, jnp....]
    cond x63 -> x0, local copies, waits for them, and re-layouts: 26.8 us -> none
    another operation x33 -> x0, loops' own time: 22.5 us -> none  [the longest x1 21.3 us: fold_piece(): return lax.fori_loop(0, shard_kv.shape[1], one_block, carried)]
    reduce_or x32 -> x0, other arithmetic: 21.4 us -> none  [block_step(): jnp.any(row_reads == 1) & present]
    reduce_sum x8 -> x1, other arithmetic: 20.5 us -> 0.91 us  [per_device(): jnp.sum(jnp.where(hit, valid_tokens[None, :], 0), axis=1)]
  transfers between devices with their start and end apart: 1 -> 1, of which waited for: 1 -> 1; matrix products, arithmetic and copies ran while one was open for 12% -> 8% of each run, Pallas kernels for 0% -> 0%
where the time goes in v1:
time: 175 us
  waiting for transfers between devices  66.4 us (38%)
  blocking collectives  50.9 us (29%)
  Pallas kernels  26.9 us (15%)
  between operations  13.4 us (8%)
  local copies, waits for them, and re-layouts  10.6 us (6%)
  other arithmetic  6.53 us (4%)
    all_gather x1, waiting for transfers between devices, per_device(): gathered = lax.all_gather(prefix_kv, 'req', axis=1, tiled=True)  65.7 us
    all_to_all x1, blocking collectives, per_device(): swapped = lax.all_to_all(context, 'head', split_axis=0, concat_axis=0)  50.9 us
    pallas_call x1, Pallas kernels, attention(): pl.pallas_call(attend, out_shape=jax.ShapeDtypeStruct(queries.shape, jnp....  26.9 us
    reshape x1, local copies, waits for them, and re-layouts, per_device(): q = queries.reshape(requests, length, local_heads * head_size)  7.34 us
  transfers between devices with their start and end apart: 1, of which 1 were waited for; matrix products, arithmetic and copies ran while one was open for 8% of the time, Pallas kernels for 0%

profile of v1, /device:TPU:0, one launch (start us, length us, event | category | flops | bytes accessed | tf_op | source)
XLA Modules:
  0.0 174.8 jit_solution(6749655218119579536)
XLA Ops:
  6.5 0.0 all-gather.2.cloned.1.call-start
  6.5 0.7 all-gather.2.cloned.1.call-update
  7.3 0.8 fusion.13
  8.1 0.9 fusion.5
  8.9 0.9 fusion.22
  9.8 0.2 fusion.6
  10.0 0.2 fusion.20
  10.2 0.2 select_reduce_fusion.5
  10.4 0.9 fusion
  11.3 0.1 copy.16
  11.4 0.1 copy.10
  11.5 0.1 copy.11
  11.6 0.1 copy.17
  11.7 0.1 copy.12
  11.8 0.1 copy.6
  11.9 0.1 copy.7
  12.0 0.1 copy.13
  12.1 0.1 copy.14
  12.2 0.1 copy.8
  12.3 0.1 copy.9
  12.4 0.1 copy.15
  12.5 1.5 reshape.200.fk_ref.fv_ref
  13.9 7.3 %reshape.199.q_ref = bf16[2,256,4096]{2,1,0:T(8,128)(2,1)} reshape(bf16[2,256,32,128]{3,2,1,0:T(8,128)(2,1)} %param.5) | data formatting | bytes 8388608 | tf_op jit(solution)/shard_map/reshape | solution.py:96
  21.3 0.1 stack.4.chosen
  21.4 0.1 stack.5.limits
  21.5 65.7 %all-gather.2.cloned.1.call-done.rest_0_.rest_1_.rest_2_.rest_3_.rest_4_.rest_5_.rest_6_.rest_7_.rest_8_.rest_9_.rest_10_.rest_11_ = bf16[2,32,4,128,128]{4,3,2,1,0:T(8,128)(2,1)} async-done(((bf16[2,2,4,128,128]{4,3,2,1,0:T(8,128)(2,1)}), bf16[2,32,4,128,128]{4,3,2,1,0:T(8,128)(2,1)}) %all-gather.2.cloned.1.call-update) | async-done | bytes 8388624 | tf_op jit(solution)/shard_map/all_gather | solution.py:83
  87.2 26.9 %shard_map.55 = bf16[2,256,4096]{2,1,0:T(8,128)(2,1)S(1)} custom-call(s32[2,6]{1,0:T(2,128)S(1)} %stack.4.chosen, s32[2,6]{1,0:T(2,128)S(1)} %stack.5.limits, bf16[2,256,4096]{2,1,0:T(8,128)(2,1)} %reshape.199.q_ref, bf16[2,2,256,512]{3,2,1,0:T(8,128)(2,1)S(1)} %reshape.200.fk_ref.fv_ref, bf16[2,2,256,512]{3,2,1,0:T(8,128)(2,1)S(1)} %reshape.200.fk_ref.fv_ref, ...), custom_call_target="tpu_custom_call" | custom-call | tf_op jit(solution)/shard_map/pallas_call | solution.py:61
  114.1 50.9 %all_to_all.5 = bf16[2,256,4096]{2,1,0:T(8,128)(2,1)S(1)} all-to-all(bf16[2,256,4096]{2,1,0:T(8,128)(2,1)S(1)} %shard_map.55), channel_id=1, replica_groups=mesh['req'=16,'head'=2] {'head'}, dimensions={0} | all-to-all | bytes 8388608 | tf_op jit(solution)/shard_map/all_to_all | solution.py:101
  165.0 0.5 slice_bitcast_fusion.1
  165.5 2.5 %pad_maximum_fusion = bf16[256,8192]{1,0:T(8,128)(2,1)} fusion(bf16[256,4096]{1,0:T(8,128)(2,1)S(1)} %get-tuple-element.16, bf16[256,4096]{1,0:T(8,128)(2,1)S(1)} %get-tuple-element.15), kind=kLoop, calls=%fused_computation | loop fusion | flops 8388608 | bytes 8388608 | tf_op jit(solution)/shard_map/concatenate | solution.py:102
  (10 shorter events, 0.1 us)
Async XLA Ops:
  6.5 80.7 %all-gather.2.cloned.1.call-start = ((), (), s32[]{:S(2)}) async-start(), calls=%async_computation.1 | async-start | bytes 8912896 | tf_op jit(solution)/shard_map/all_gather | solution.py:83
Sparse Core Ops, SparseCore 0:
  9.6 77.6 all-gather.1

commit v2 on v1

--- a/solution.py
+++ b/solution.py
@@ -80,7 +80,6 @@
 def per_device(queries, fresh_key_value, prefix_kv, block_mask, valid_tokens):
     requests, length, local_heads, head_size = queries.shape
     blocks = block_mask.shape[1]
-    gathered = lax.all_gather(prefix_kv, "req", axis=1, tiled=True)
     order = blocks - jnp.arange(blocks, dtype=jnp.int32)
     ranking = jnp.where(block_mask == 1, order, 0)
     chosen, limits = [], []
@@ -93,13 +92,22 @@
         ranking = jnp.where(hit, 0, ranking)
     chosen = jnp.stack(chosen, axis=1).astype(jnp.int32)
     limits = jnp.stack(limits, axis=1).astype(jnp.int32)
-    q = queries.reshape(requests, length, local_heads * head_size)
-    fresh = fresh_key_value.reshape(2, requests, length, -1)
-    context = attention(q, fresh, gathered, chosen, limits)
+    local_kv = fresh_key_value.shape[3]
+    group = local_heads // local_kv
     parts = lax.axis_size("head")
-    context = context.reshape(parts, requests * length // parts, local_heads * head_size)
-    swapped = lax.all_to_all(context, "head", split_axis=0, concat_axis=0)
-    return jnp.concatenate([swapped[i] for i in range(parts)], axis=1)
+    rows = requests * length // parts
+    gathered = [
+        lax.all_gather(prefix_kv[:, :, k : k + 1], "req", axis=1, tiled=True)
+        for k in range(local_kv)
+    ]
+    pieces = []
+    for k in range(local_kv):
+        q = queries[:, :, k * group : (k + 1) * group].reshape(requests, length, group * head_size)
+        fresh = fresh_key_value[:, :, :, k]
+        context = attention(q, fresh, gathered[k], chosen, limits)
+        context = context.reshape(parts, rows, group * head_size)
+        pieces.append(lax.all_to_all(context, "head", split_axis=0, concat_axis=0))
+    return jnp.concatenate([piece[i] for i in range(parts) for piece in pieces], axis=1)
 
 
 def solution(mesh):

time: 175 us -> 220 us (1.26)
  waiting for transfers between devices: 66.4 us -> 124 us
  blocking collectives: 50.9 us -> 0 us
  local copies, waits for them, and re-layouts: 10.6 us -> 33.3 us
  starting transfers between devices: 0.01 us -> 15.5 us
  other arithmetic: 6.53 us -> 4.08 us
    all_to_all x1 -> x0, blocking collectives: 50.9 us -> none  [per_device(): swapped = lax.all_to_all(context, 'head', split_axis=0, concat_axis=0)]
    all_gather x1 -> x4, waiting for transfers between devices: 65.7 us -> 112 us  [per_device(): lax.all_gather(prefix_kv[:, :, k:k + 1], 'req', axis=1, tiled=True)]
    unnamed x0 -> x21, local copies, waits for them, and re-layouts: none -> 17.5 us
    all_to_all x0 -> x4, starting transfers between devices: none -> 15.3 us  [per_device(): pieces.append(lax.all_to_all(context, 'head', split_axis=0, concat_axis=0))]
    all_to_all x0 -> x4, waiting for transfers between devices: none -> 10.8 us  [per_device(): pieces.append(lax.all_to_all(context, 'head', split_axis=0, concat_axis=0))]
    slice x0 -> x3, local copies, waits for them, and re-layouts: none -> 8.57 us  [the longest x1 4.14 us: per_device(): queries[:, :, k * group:(k + 1) * group]]
    reshape x2 -> x4, local copies, waits for them, and re-layouts: 8.81 us -> 5.06 us  [per_device(): queries[:, :, k * group:(k + 1) * group]]
    concatenate x1 -> x0, other arithmetic: 2.46 us -> none  [per_device(): return jnp.concatenate([swapped[i] for i in range(parts)], axis=1)]
  transfers between devices with their start and end apart: 1 -> 8, of which waited for: 1 -> 5; matrix products, arithmetic and copies ran while one was open for 8% -> 11% of each run, Pallas kernels for 0% -> 13%
where the time goes in v2:
time: 220 us; the launch traced here: 219 us
  waiting for transfers between devices  124 us (56%)
  local copies, waits for them, and re-layouts  33.3 us (15%)
  Pallas kernels  28.8 us (13%)
  starting transfers between devices  15.5 us (7%)
  between operations  13.2 us (6%)
  other arithmetic  4.08 us (2%)
    all_gather x4, waiting for transfers between devices, per_device(): lax.all_gather(prefix_kv[:, :, k:k + 1], 'req', axis=1, tiled=True)  112 us
    pallas_call x4, Pallas kernels, attention(): pl.pallas_call(attend, out_shape=jax.ShapeDtypeStruct(queries.shape, jnp....  28.8 us
    unnamed x21, local copies, waits for them, and re-layouts  17.5 us
    all_to_all x4, starting transfers between devices, per_device(): pieces.append(lax.all_to_all(context, 'head', split_axis=0, concat_axis=0))  15.3 us
    all_to_all x4, waiting for transfers between devices, per_device(): pieces.append(lax.all_to_all(context, 'head', split_axis=0, concat_axis=0))  10.8 us
    reshape x4, local copies, waits for them, and re-layouts, per_device(): queries[:, :, k * group:(k + 1) * group]  5.06 us
  transfers between devices with their start and end apart: 8, of which 5 were waited for; matrix products, arithmetic and copies ran while one was open for 11% of the time, Pallas kernels for 13%

profile of v2, /device:TPU:0, one launch (start us, length us, event | category | flops | bytes accessed | tf_op | source)
XLA Modules:
  0.0 219.1 jit_solution(3173931212432959705)
XLA Ops:
  6.5 1.9 fusion.34
  11.4 0.9 fusion.13
  12.2 0.9 fusion.30
  13.7 0.9 fusion.8
  15.7 4.1 %fusion.32 = (bf16[2,256,8,128]{3,2,1,0:T(8,128)(2,1)}, bf16[2,256,8,128]{3,2,1,0:T(8,128)(2,1)S(1)}, bf16[2,256,8,128]{3,2,1,0:T(8,128)(2,1)}, bf16[2,256,8,128]{3,2,1,0:T(8,128)(2,1)}) fusion(bf16[2,256,32,128]{3,2,1,0:T(8,128)(2,1)} %param.5), kind=kLoop, calls=%fused_computation.68 | loop fusion | bytes 8388608 | tf_op jit(solution)/shard_map/slice | solution.py:105
  19.9 1.5 reshape.205.q_ref
  21.4 2.5 %fusion.33 = (bf16[2,2,256,1,128]{4,3,2,1,0:T(2,128)(2,1)}, bf16[2,2,256,1,128]{4,3,2,1,0:T(2,128)(2,1)}, bf16[2,2,256,1,128]{4,3,2,1,0:T(2,128)(2,1)}, bf16[2,2,256,1,128]{4,3,2,1,0:T(2,128)(2,1)S(1)}) fusion(bf16[2,2,256,4,128]{4,3,2,1,0:T(4,128)(2,1)S(1)} %copy-done.4), kind=kLoop, calls=%fused_computation.69 | loop fusion | bytes 2097152 | tf_op jit(solution)/shard_map/slice | solution.py:106
  24.2 29.5 %all-gather.5.cloned.1.call-done.rest_0_.rest_1_.rest_2_.rest_3_.rest_4_.rest_5_.rest_6_.rest_7_.rest_8_.rest_9_.rest_10_.rest_11_ = bf16[2,32,1,128,128]{4,3,2,1,0:T(8,128)(2,1)} async-done(((bf16[2,2,1,128,128]{4,3,2,1,0:T(8,128)(2,1)}), bf16[2,32,1,128,128]{4,3,2,1,0:T(8,128)(2,1)}) %all-gather.5.cloned.1.call-update) | async-done | bytes 2097168 | tf_op jit(solution)/shard_map/all_gather | solution.py:100
  53.6 1.6 copy-done.3
  55.2 7.2 %shard_map.55 = bf16[2,256,1024]{2,1,0:T(8,128)(2,1)} custom-call(s32[2,6]{1,0:T(2,128)S(1)} %stack.4.chosen, s32[2,6]{1,0:T(2,128)S(1)} %stack.5.limits, bf16[2,256,1024]{2,1,0:T(8,128)(2,1)S(1)} %reshape.205.q_ref, bf16[2,2,256,128]{3,2,1,0:T(8,128)(2,1)S(1)} %bitcast.76, bf16[2,2,256,128]{3,2,1,0:T(8,128)(2,1)S(1)} %bitcast.77, ...), custom_call_target="tpu_custom_call" | custom-call | tf_op jit(solution)/shard_map/pallas_call | solution.py:61
  62.4 3.6 %all-to-all-start = ((bf16[2,256,1024]{2,1,0:T(8,128)(2,1)}), bf16[2,256,1024]{2,1,0:T(8,128)(2,1)S(1)}, u32[]{:S(2)}, u32[]{:S(2)}) async-start(bf16[2,256,1024]{2,1,0:T(8,128)(2,1)} %shard_map.55), calls=%async_computation | async-start | bytes 2097152 | tf_op jit(solution)/shard_map/all_to_all | solution.py:109
  66.5 1.1 copy.32
  67.6 28.5 %all-gather.7.cloned.1.call-done.rest_0_.rest_1_.rest_2_.rest_3_.rest_4_.rest_5_.rest_6_.rest_7_.rest_8_.rest_9_.rest_10_.rest_11_ = bf16[2,32,1,128,128]{4,3,2,1,0:T(8,128)(2,1)} async-done(((bf16[2,2,1,128,128]{4,3,2,1,0:T(8,128)(2,1)}), bf16[2,32,1,128,128]{4,3,2,1,0:T(8,128)(2,1)}) %all-gather.7.cloned.1.call-update) | async-done | bytes 2097168 | tf_op jit(solution)/shard_map/all_gather | solution.py:100
  96.0 1.6 copy-done.2
  97.6 7.2 %shard_map.56 = bf16[2,256,1024]{2,1,0:T(8,128)(2,1)} custom-call(s32[2,6]{1,0:T(2,128)S(1)} %stack.4.chosen, s32[2,6]{1,0:T(2,128)S(1)} %stack.5.limits, bf16[2,256,1024]{2,1,0:T(8,128)(2,1)S(1)} %reshape.206.q_ref, bf16[2,2,256,128]{3,2,1,0:T(8,128)(2,1)S(1)} %bitcast.80, bf16[2,2,256,128]{3,2,1,0:T(8,128)(2,1)S(1)} %bitcast.81, ...), custom_call_target="tpu_custom_call" | custom-call | tf_op jit(solution)/shard_map/pallas_call | solution.py:61
  104.9 3.6 %all-to-all-start.1 = ((bf16[2,256,1024]{2,1,0:T(8,128)(2,1)}), bf16[2,256,1024]{2,1,0:T(8,128)(2,1)S(1)}, u32[]{:S(2)}, u32[]{:S(2)}) async-start(bf16[2,256,1024]{2,1,0:T(8,128)(2,1)} %shard_map.56), calls=%async_computation.1 | async-start | bytes 2097152 | tf_op jit(solution)/shard_map/all_to_all | solution.py:109
  108.4 1.5 reshape.207.q_ref
  110.0 1.1 copy.31
  111.1 27.4 %all-gather.9.cloned.1.call-done.rest_0_.rest_1_.rest_2_.rest_3_.rest_4_.rest_5_.rest_6_.rest_7_.rest_8_.rest_9_.rest_10_.rest_11_ = bf16[2,32,1,128,128]{4,3,2,1,0:T(8,128)(2,1)} async-done(((bf16[2,2,1,128,128]{4,3,2,1,0:T(8,128)(2,1)}), bf16[2,32,1,128,128]{4,3,2,1,0:T(8,128)(2,1)}) %all-gather.9.cloned.1.call-update) | async-done | bytes 2097168 | tf_op jit(solution)/shard_map/all_gather | solution.py:100
  138.5 1.6 copy-done.1
  140.1 7.2 %shard_map.57 = bf16[2,256,1024]{2,1,0:T(8,128)(2,1)} custom-call(s32[2,6]{1,0:T(2,128)S(1)} %stack.4.chosen, s32[2,6]{1,0:T(2,128)S(1)} %stack.5.limits, bf16[2,256,1024]{2,1,0:T(8,128)(2,1)S(1)} %reshape.207.q_ref, bf16[2,2,256,128]{3,2,1,0:T(8,128)(2,1)S(1)} %bitcast.82, bf16[2,2,256,128]{3,2,1,0:T(8,128)(2,1)S(1)} %bitcast.83, ...), custom_call_target="tpu_custom_call" | custom-call | tf_op jit(solution)/shard_map/pallas_call | solution.py:61
  147.3 4.6 %all-to-all-start.2 = ((bf16[2,256,1024]{2,1,0:T(8,128)(2,1)}), bf16[2,256,1024]{2,1,0:T(8,128)(2,1)}, u32[]{:S(2)}, u32[]{:S(2)}) async-start(bf16[2,256,1024]{2,1,0:T(8,128)(2,1)} %shard_map.57), calls=%async_computation.2 | async-start | bytes 2097152 | tf_op jit(solution)/shard_map/all_to_all | solution.py:109
  151.9 1.5 reshape.208.q_ref
  153.4 1.1 copy.30
  154.5 26.3 %all-gather.11.cloned.1.call-done.rest_0_.rest_1_.rest_2_.rest_3_.rest_4_.rest_5_.rest_6_.rest_7_.rest_8_.rest_9_.rest_10_.rest_11_ = bf16[2,32,1,128,128]{4,3,2,1,0:T(8,128)(2,1)} async-done(((bf16[2,2,1,128,128]{4,3,2,1,0:T(8,128)(2,1)}), bf16[2,32,1,128,128]{4,3,2,1,0:T(8,128)(2,1)}) %all-gather.11.cloned.1.call-update) | async-done | bytes 2097168 | tf_op jit(solution)/shard_map/all_gather | solution.py:100
  180.8 1.6 copy-done
  182.3 7.2 %shard_map.58 = bf16[2,256,1024]{2,1,0:T(8,128)(2,1)} custom-call(s32[2,6]{1,0:T(2,128)S(1)} %stack.4.chosen, s32[2,6]{1,0:T(2,128)S(1)} %stack.5.limits, bf16[2,256,1024]{2,1,0:T(8,128)(2,1)S(1)} %reshape.208.q_ref, bf16[2,2,256,128]{3,2,1,0:T(8,128)(2,1)S(1)} %bitcast.78, bf16[2,2,256,128]{3,2,1,0:T(8,128)(2,1)S(1)} %bitcast.79, ...), custom_call_target="tpu_custom_call" | custom-call | tf_op jit(solution)/shard_map/pallas_call | solution.py:61
  189.6 3.6 %all-to-all-start.3 = ((bf16[2,256,1024]{2,1,0:T(8,128)(2,1)}), bf16[2,256,1024]{2,1,0:T(8,128)(2,1)S(1)}, u32[]{:S(2)}, u32[]{:S(2)}) async-start(bf16[2,256,1024]{2,1,0:T(8,128)(2,1)} %shard_map.58), calls=%async_computation.3 | async-start | bytes 2097152 | tf_op jit(solution)/shard_map/all_to_all | solution.py:109
  193.2 0.8 fusion.7
  194.8 1.9 fusion.5
  196.7 10.8 %all-to-all-done.3 = bf16[2,256,1024]{2,1,0:T(8,128)(2,1)S(1)} async-done(((bf16[2,256,1024]{2,1,0:T(8,128)(2,1)}), bf16[2,256,1024]{2,1,0:T(8,128)(2,1)S(1)}, u32[]{:S(2)}, u32[]{:S(2)}) %all-to-all-start.3) | async-done | bytes 1048608 | tf_op jit(solution)/shard_map/all_to_all | solution.py:109
  209.9 1.9 fusion.1
  (52 shorter events, 9.4 us)
Async XLA Ops:
  6.5 47.1 %all-gather.5.cloned.1.call-start = ((), (), s32[]{:S(2)}) async-start(), calls=%async_computation.4 | async-start | bytes 2228224 | tf_op jit(solution)/shard_map/all_gather | solution.py:100
  8.5 87.6 %all-gather.7.cloned.1.call-start = ((), (), s32[]{:S(2)}) async-start(), calls=%async_computation.5 | async-start | bytes 2228224 | tf_op jit(solution)/shard_map/all_gather | solution.py:100
  9.2 129.2 %all-gather.9.cloned.1.call-start = ((), (), s32[]{:S(2)}) async-start(), calls=%async_computation.6 | async-start | bytes 2228224 | tf_op jit(solution)/shard_map/all_gather | solution.py:100
  10.0 170.8 %all-gather.11.cloned.1.call-start = ((), (), s32[]{:S(2)}) async-start(), calls=%async_computation.7 | async-start | bytes 2228224 | tf_op jit(solution)/shard_map/all_gather | solution.py:100
  15.7 5.7 %copy-start.4 = (bf16[2,2,256,4,128]{4,3,2,1,0:T(4,128)(2,1)S(1)}, bf16[2,2,256,4,128]{4,3,2,1,0:T(4,128)(2,1)}, u32[]{:S(2)}) copy-start(bf16[2,2,256,4,128]{4,3,2,1,0:T(4,128)(2,1)} %param.6) | copy-start | bytes 3145732
  53.6 1.6 copy-start.3
  62.4 42.5 %all-to-all-start = ((bf16[2,256,1024]{2,1,0:T(8,128)(2,1)}), bf16[2,256,1024]{2,1,0:T(8,128)(2,1)S(1)}, u32[]{:S(2)}, u32[]{:S(2)}) async-start(bf16[2,256,1024]{2,1,0:T(8,128)(2,1)} %shard_map.55), calls=%async_computation | async-start | bytes 2097152 | tf_op jit(solution)/shard_map/all_to_all | solution.py:109
  96.0 1.6 copy-start.2
  104.9 42.4 %all-to-all-start.1 = ((bf16[2,256,1024]{2,1,0:T(8,128)(2,1)}), bf16[2,256,1024]{2,1,0:T(8,128)(2,1)S(1)}, u32[]{:S(2)}, u32[]{:S(2)}) async-start(bf16[2,256,1024]{2,1,0:T(8,128)(2,1)} %shard_map.56), calls=%async_computation.1 | async-start | bytes 2097152 | tf_op jit(solution)/shard_map/all_to_all | solution.py:109
  138.5 1.6 copy-start.1
  147.3 42.3 %all-to-all-start.2 = ((bf16[2,256,1024]{2,1,0:T(8,128)(2,1)}), bf16[2,256,1024]{2,1,0:T(8,128)(2,1)}, u32[]{:S(2)}, u32[]{:S(2)}) async-start(bf16[2,256,1024]{2,1,0:T(8,128)(2,1)} %shard_map.57), calls=%async_computation.2 | async-start | bytes 2097152 | tf_op jit(solution)/shard_map/all_to_all | solution.py:109
  180.8 1.6 copy-start
  189.6 17.9 %all-to-all-start.3 = ((bf16[2,256,1024]{2,1,0:T(8,128)(2,1)}), bf16[2,256,1024]{2,1,0:T(8,128)(2,1)S(1)}, u32[]{:S(2)}, u32[]{:S(2)}) async-start(bf16[2,256,1024]{2,1,0:T(8,128)(2,1)} %shard_map.58), calls=%async_computation.3 | async-start | bytes 2097152 | tf_op jit(solution)/shard_map/all_to_all | solution.py:109
Sparse Core Ops, SparseCore 0:
  9.5 44.0 all-gather.4
  55.8 40.1 all-gather.6
  98.2 40.1 all-gather.8
  140.5 40.1 all-gather.10

commit v3 on v2

--- a/solution.py
+++ b/solution.py
@@ -10,6 +10,7 @@
 
 PATH = 6
 MASKED = -1e30
+MESH = pl.DeviceIdType.MESH
 
 
 def attend(chosen, limits, q_ref, fk_ref, fv_ref, *rest):
@@ -22,10 +23,10 @@
 
     row = lax.broadcasted_iota(jnp.int32, (slots, width), 0)
     marks = [jnp.where(row < limits[r, j], 0.0, MASKED).astype(jnp.bfloat16) for j in range(PATH)]
-    keys = jnp.concatenate([k[0, 0, 0] for k in k_refs] + [fk_ref[0, 0]], axis=0)
+    keys = jnp.concatenate([k[0, 0, 0, 0] for k in k_refs] + [fk_ref[0, 0]], axis=0)
     marks = jnp.concatenate(marks + [jnp.zeros((tokens, width), jnp.bfloat16)], axis=0)
     keys = jnp.concatenate([keys, marks], axis=1)
-    values = jnp.concatenate([v[0, 0, 0] for v in v_refs] + [fv_ref[0, 0]], axis=0)
+    values = jnp.concatenate([v[0, 0, 0, 0] for v in v_refs] + [fv_ref[0, 0]], axis=0)
     values = jnp.concatenate([values, jnp.ones_like(values)], axis=1)
     first = (lax.broadcasted_iota(jnp.int32, (tokens, width), 1) == 0).astype(jnp.bfloat16)
     later = lax.broadcasted_iota(jnp.int32, (tokens, tokens), 0) < lax.broadcasted_iota(
@@ -46,28 +47,164 @@
         out_ref[0, :, cols] = (both[:, :width] / both[:, width:]).astype(jnp.bfloat16)
 
 
-def attention(queries, fresh, prefix, chosen, limits):
-    requests, tokens, heads_wide = queries.shape
-    local_kv, slots, width = prefix.shape[2:]
-    wide = heads_wide // local_kv
+def gather_kernel(columns, src, out, up_sem, down_sem, x_sem, near_sem, far_sem, recv_sem, own_sem):
+    me = lax.axis_index("req")
+    core, x, z = me % 2, (me // 2) % 2, me // 4
+    last = columns - 1
+
+    def at(z_at, x_at, core_at):
+        return z_at * 4 + x_at * 2 + core_at
+
+    barrier = pltpu.get_barrier_semaphore()
+
+    def greet(device):
+        pl.semaphore_signal(barrier, inc=1, device_id={"req": device}, device_id_type=MESH)
+
+    greet(at(z, x, 1 - core))
+    greet(at(z, 1 - x, core))
+
+    @pl.when(z > 0)
+    def _():
+        greet(me - 4)
+
+    @pl.when(z < last)
+    def _():
+        greet(me + 4)
+
+    peers = 2 + (z > 0).astype(jnp.int32) + (z < last).astype(jnp.int32)
+    pl.semaphore_wait(barrier, peers)
+
+    def copy(shard, send_sem, device, from_src=False):
+        return pltpu.make_async_remote_copy(
+            src_ref=src if from_src else out.at[shard],
+            dst_ref=out.at[shard],
+            send_sem=send_sem,
+            recv_sem=recv_sem.at[shard],
+            device_id={"req": device},
+            device_id_type=MESH,
+        )
+
+    def arrived(shard):
+        copy(shard, x_sem.at[0], at(z, 1 - x, core)).wait_recv()
+
+    def always(action):
+        action()
+
+    column = [(0, z, None, True)]
+    for d in range(1, columns):
+        column.append((d, z - d, z >= d, False))
+        column.append((columns - 1 + d, z + d, z + d <= last, False))
+
+    def when(condition):
+        return always if condition is None else pl.when(condition)
+
+    def z_sends(slot, z_at, from_src):
+        shard = at(z_at, x, core)
+        found = []
+        if slot < columns:
+            found.append((z < last, copy(shard, up_sem.at[slot], me + 4, from_src)))
+        if slot == 0 or slot >= columns:
+            found.append((z > 0, copy(shard, down_sem.at[slot], me - 4, from_src)))
+        return found
+
+    def spread(slot, z_at, from_src):
+        shard = at(z_at, x, core)
+        return [
+            copy(shard, x_sem.at[slot], at(z, 1 - x, core), from_src),
+            copy(shard, near_sem.at[slot], at(z, x, 1 - core), from_src),
+        ]
+
+    def relay(slot, z_at):
+        shard = at(z_at, 1 - x, core)
+        return shard, copy(shard, far_sem.at[slot], at(z, x, 1 - core))
+
+    def step_column(entry):
+        slot, z_at, condition, own = entry
+
+        @when(condition)
+        def _():
+            if not own:
+                arrived(at(z_at, x, core))
+            for also, send in z_sends(slot, z_at, own):
+                pl.when(also)(send.start)
+            for send in spread(slot, z_at, own):
+                send.start()
+
+    def step_far(entry):
+        slot, z_at, condition, _ = entry
+
+        @when(condition)
+        def _():
+            shard, send = relay(slot, z_at)
+            arrived(shard)
+            send.start()
+
+    keep = pltpu.make_async_copy(src, out.at[me], own_sem)
+    step_column(column[0])
+    keep.start()
+    for d in range(1, columns):
+        for entry in column[2 * d - 1 : 2 * d + 1]:
+            step_column(entry)
+        for entry in column[max(2 * d - 3, 0) : 2 * d - 1]:
+            step_far(entry)
+    for entry in column[-2:]:
+        step_far(entry)
+
+    for slot, z_at, condition, own in column:
+
+        @when(condition)
+        def _(slot=slot, z_at=z_at, own=own):
+            arrived(at(z_at, x, 1 - core))
+            arrived(at(z_at, 1 - x, 1 - core))
+            for also, send in z_sends(slot, z_at, own):
+                pl.when(also)(send.wait_send)
+            for send in spread(slot, z_at, own):
+                send.wait_send()
+            relay(slot, z_at)[1].wait_send()
+
+    keep.wait()
+
+
+def gather(prefix):
+    devices = lax.axis_size("req")
+    columns = devices // 4
+    slots = 2 * columns - 1
+    dma = pltpu.SemaphoreType.DMA
+    return pl.pallas_call(
+        functools.partial(gather_kernel, columns),
+        out_shape=jax.ShapeDtypeStruct((devices,) + prefix.shape, prefix.dtype),
+        in_specs=[pl.BlockSpec(memory_space=pl.ANY)],
+        out_specs=pl.BlockSpec(memory_space=pl.ANY),
+        scratch_shapes=[dma((slots,))] * 5 + [dma((devices,)), dma],
+        compiler_params=pltpu.CompilerParams(collective_id=1, has_side_effects=True),
+    )(prefix)
+
+
+def attention(queries, fresh, prefix, chosen, limits, head):
+    requests, tokens, wide = queries.shape
+    blocks_dev = prefix.shape[2]
+    slots, width = prefix.shape[-2:]
 
     def block_map(kv, j):
-        return lambda r, k, chosen, limits: (kv, chosen[r, j], k, 0, 0)
+        def place(r, chosen, limits):
+            return (chosen[r, j] // blocks_dev, kv, chosen[r, j] % blocks_dev, head, 0, 0)
+
+        return place
 
     def fresh_map(kv):
-        return lambda r, k, chosen, limits: (kv, r, 0, k)
-
-    q_spec = pl.BlockSpec((1, tokens, wide), lambda r, k, chosen, limits: (r, 0, k))
+        return lambda r, chosen, limits: (kv, r, 0, 0)
+
+    q_spec = pl.BlockSpec((1, tokens, wide), lambda r, chosen, limits: (r, 0, 0))
     return pl.pallas_call(
         attend,
         out_shape=jax.ShapeDtypeStruct(queries.shape, jnp.bfloat16),
         grid_spec=pltpu.PrefetchScalarGridSpec(
             num_scalar_prefetch=2,
-            grid=(requests, local_kv),
+            grid=(requests,),
             in_specs=[q_spec]
             + [pl.BlockSpec((1, 1, tokens, width), fresh_map(kv)) for kv in (0, 1)]
             + [
-                pl.BlockSpec((1, 1, 1, slots, width), block_map(kv, j))
+                pl.BlockSpec((1, 1, 1, 1, slots, width), block_map(kv, j))
                 for kv in (0, 1)
                 for j in range(PATH)
             ],
@@ -96,15 +233,12 @@
     group = local_heads // local_kv
     parts = lax.axis_size("head")
     rows = requests * length // parts
-    gathered = [
-        lax.all_gather(prefix_kv[:, :, k : k + 1], "req", axis=1, tiled=True)
-        for k in range(local_kv)
-    ]
+    gathered = gather(prefix_kv)
     pieces = []
     for k in range(local_kv):
         q = queries[:, :, k * group : (k + 1) * group].reshape(requests, length, group * head_size)
         fresh = fresh_key_value[:, :, :, k]
-        context = attention(q, fresh, gathered[k], chosen, limits)
+        context = attention(q, fresh, gathered, chosen, limits, k)
         context = context.reshape(parts, rows, group * head_size)
         pieces.append(lax.all_to_all(context, "head", split_axis=0, concat_axis=0))
     return jnp.concatenate([piece[i] for i in range(parts) for piece in pieces], axis=1)

time: 220 us -> 154 us (0.70)
  waiting for transfers between devices: 124 us -> 15.8 us
  Pallas kernels: 28.8 us -> 91.4 us
  between operations: 13.2 us -> 0.13 us
  local copies, waits for them, and re-layouts: 33.3 us -> 25.6 us
    all_gather x4 -> x0, waiting for transfers between devices: 112 us -> none  [per_device(): lax.all_gather(prefix_kv[:, :, k:k + 1], 'req', axis=1, tiled=True)]
    pallas_call x0 -> x1, Pallas kernels: none -> 56.6 us  [gather(): pl.pallas_call(functools.partial(gather_kernel, columns), out_shape=jax.S...]
    unnamed x21 -> x13, local copies, waits for them, and re-layouts: 17.5 us -> 11.1 us
    pallas_call x4, Pallas kernels: 28.8 us -> 34.8 us  [attention(): pl.pallas_call(attend, out_shape=jax.ShapeDtypeStruct(queries.shape, jnp....]
    all_to_all x4, waiting for transfers between devices: 10.8 us -> 15.8 us  [per_device(): pieces.append(lax.all_to_all(context, 'head', split_axis=0, concat_axis=0))]
    slice x1, local copies, waits for them, and re-layouts: 2.52 us -> 5.17 us  [per_device(): fresh = fresh_key_value[:, :, :, k]]
  transfers between devices with their start and end apart: 8 -> 4, of which waited for: 5 -> 4; matrix products, arithmetic and copies ran while one was open for 11% -> 7% of each run, Pallas kernels for 13% -> 17%
where the time goes in v3:
time: 154 us; the launch traced here: 152 us
  Pallas kernels  91.4 us (59%)
  local copies, waits for them, and re-layouts  25.6 us (17%)
  waiting for transfers between devices  15.8 us (10%)
  starting transfers between devices  15.4 us (10%)
  other arithmetic  4.06 us (3%)
    pallas_call x1, Pallas kernels, gather(): pl.pallas_call(functools.partial(gather_kernel, columns), out_shape=jax.S...  56.6 us
    pallas_call x4, Pallas kernels, attention(): pl.pallas_call(attend, out_shape=jax.ShapeDtypeStruct(queries.shape, jnp....  34.8 us
    all_to_all x4, waiting for transfers between devices, per_device(): pieces.append(lax.all_to_all(context, 'head', split_axis=0, concat_axis=0))  15.8 us
    all_to_all x4, starting transfers between devices, per_device(): pieces.append(lax.all_to_all(context, 'head', split_axis=0, concat_axis=0))  15.4 us
    unnamed x13, local copies, waits for them, and re-layouts  11.1 us
    slice x1, local copies, waits for them, and re-layouts, per_device(): fresh = fresh_key_value[:, :, :, k]  5.17 us
    reshape x4, local copies, waits for them, and re-layouts, per_device(): queries[:, :, k * group:(k + 1) * group]  5.05 us
    reduce_max x6, other arithmetic, per_device(): best = jnp.max(ranking, axis=1)  3.09 us
  transfers between devices with their start and end apart: 4, of which 4 were waited for; matrix products, arithmetic and copies ran while one was open for 7% of the time, Pallas kernels for 17%

profile of v3, /device:TPU:0, one launch (start us, length us, event | category | flops | bytes accessed | tf_op | source)
XLA Modules:
  0.0 152.4 jit_solution(593615689134479620)
XLA Ops:
  0.8 0.9 fusion.13
  1.7 0.9 fusion.30
  3.1 0.9 fusion.8
  5.2 5.2 %fusion.33 = (bf16[2,2,256,1,128]{4,3,2,1,0:T(2,128)(2,1)}, bf16[2,2,256,1,128]{4,3,2,1,0:T(2,128)(2,1)}, bf16[2,2,256,1,128]{4,3,2,1,0:T(2,128)(2,1)}, bf16[2,2,256,1,128]{4,3,2,1,0:T(2,128)(2,1)S(1)}) fusion(bf16[2,2,256,4,128]{4,3,2,1,0:T(4,128)(2,1)} %param.6), kind=kLoop, calls=%fused_computation.69 | loop fusion | bytes 2097152 | tf_op jit(solution)/shard_map/slice | solution.py:240
  10.4 2.1 %fusion.32 = (bf16[2,256,8,128]{3,2,1,0:T(8,128)(2,1)}, bf16[2,256,8,128]{3,2,1,0:T(8,128)(2,1)S(1)}, bf16[2,256,8,128]{3,2,1,0:T(8,128)(2,1)}, bf16[2,256,8,128]{3,2,1,0:T(8,128)(2,1)}) fusion(bf16[2,256,32,128]{3,2,1,0:T(8,128)(2,1)S(1)} %copy-done), kind=kLoop, calls=%fused_computation.68 | loop fusion | bytes 8388608 | tf_op jit(solution)/shard_map/slice | solution.py:239
  12.6 1.5 reshape.205.q_ref
  14.1 56.6 %shard_map.55.rest_0_.rest_1_.rest_2_.rest_3_.rest_4_.rest_5_.rest_6_.rest_7_.rest_8_.rest_9_.rest_10_.rest_11_ = bf16[16,2,2,4,128,128]{5,4,3,2,1,0:T(8,128)(2,1)} custom-call(bf16[2,2,4,128,128]{4,3,2,1,0:T(8,128)(2,1)} %src.1), custom_call_target="tpu_custom_call" | custom-call | tf_op jit(solution)/shard_map/pallas_call | solution.py:173
  70.9 8.6 %shard_map.56 = bf16[2,256,1024]{2,1,0:T(8,128)(2,1)} custom-call(s32[2,6]{1,0:T(2,128)S(1)} %stack.4.chosen, s32[2,6]{1,0:T(2,128)S(1)} %stack.5.limits, bf16[2,256,1024]{2,1,0:T(8,128)(2,1)S(1)} %reshape.205.q_ref, bf16[2,2,256,128]{3,2,1,0:T(8,128)(2,1)S(1)} %bitcast.76, bf16[2,2,256,128]{3,2,1,0:T(8,128)(2,1)S(1)} %bitcast.77, ...), custom_call_target="tpu_custom_call" | custom-call | tf_op jit(solution)/shard_map/pallas_call | solution.py:198
  79.5 3.6 %all-to-all-start = ((bf16[2,256,1024]{2,1,0:T(8,128)(2,1)}), bf16[2,256,1024]{2,1,0:T(8,128)(2,1)S(1)}, u32[]{:S(2)}, u32[]{:S(2)}) async-start(bf16[2,256,1024]{2,1,0:T(8,128)(2,1)} %shard_map.56), calls=%async_computation | async-start | bytes 2097152 | tf_op jit(solution)/shard_map/all_to_all | solution.py:243
  83.1 1.1 copy.32
  84.7 8.7 %shard_map.57 = bf16[2,256,1024]{2,1,0:T(8,128)(2,1)} custom-call(s32[2,6]{1,0:T(2,128)S(1)} %stack.4.chosen, s32[2,6]{1,0:T(2,128)S(1)} %stack.5.limits, bf16[2,256,1024]{2,1,0:T(8,128)(2,1)S(1)} %reshape.206.q_ref, bf16[2,2,256,128]{3,2,1,0:T(8,128)(2,1)S(1)} %bitcast.80, bf16[2,2,256,128]{3,2,1,0:T(8,128)(2,1)S(1)} %bitcast.81, ...), custom_call_target="tpu_custom_call" | custom-call | tf_op jit(solution)/shard_map/pallas_call | solution.py:198
  93.4 4.1 %all-to-all-done = bf16[2,256,1024]{2,1,0:T(8,128)(2,1)S(1)} async-done(((bf16[2,256,1024]{2,1,0:T(8,128)(2,1)}), bf16[2,256,1024]{2,1,0:T(8,128)(2,1)S(1)}, u32[]{:S(2)}, u32[]{:S(2)}) %all-to-all-start) | async-done | bytes 1048608 | tf_op jit(solution)/shard_map/all_to_all | solution.py:243
  97.5 3.8 %all-to-all-start.1 = ((bf16[2,256,1024]{2,1,0:T(8,128)(2,1)}), bf16[2,256,1024]{2,1,0:T(8,128)(2,1)S(1)}, u32[]{:S(2)}, u32[]{:S(2)}) async-start(bf16[2,256,1024]{2,1,0:T(8,128)(2,1)} %shard_map.57), calls=%async_computation.1 | async-start | bytes 2097152 | tf_op jit(solution)/shard_map/all_to_all | solution.py:243
  101.3 1.1 copy.31
  102.3 1.5 reshape.207.q_ref
  103.9 8.7 %shard_map.58 = bf16[2,256,1024]{2,1,0:T(8,128)(2,1)} custom-call(s32[2,6]{1,0:T(2,128)S(1)} %stack.4.chosen, s32[2,6]{1,0:T(2,128)S(1)} %stack.5.limits, bf16[2,256,1024]{2,1,0:T(8,128)(2,1)S(1)} %reshape.207.q_ref, bf16[2,2,256,128]{3,2,1,0:T(8,128)(2,1)S(1)} %bitcast.82, bf16[2,2,256,128]{3,2,1,0:T(8,128)(2,1)S(1)} %bitcast.83, ...), custom_call_target="tpu_custom_call" | custom-call | tf_op jit(solution)/shard_map/pallas_call | solution.py:198
  112.6 2.1 %all-to-all-done.1 = bf16[2,256,1024]{2,1,0:T(8,128)(2,1)S(1)} async-done(((bf16[2,256,1024]{2,1,0:T(8,128)(2,1)}), bf16[2,256,1024]{2,1,0:T(8,128)(2,1)S(1)}, u32[]{:S(2)}, u32[]{:S(2)}) %all-to-all-start.1) | async-done | bytes 1048608 | tf_op jit(solution)/shard_map/all_to_all | solution.py:243
  114.7 4.5 %all-to-all-start.2 = ((bf16[2,256,1024]{2,1,0:T(8,128)(2,1)}), bf16[2,256,1024]{2,1,0:T(8,128)(2,1)}, u32[]{:S(2)}, u32[]{:S(2)}) async-start(bf16[2,256,1024]{2,1,0:T(8,128)(2,1)} %shard_map.58), calls=%async_computation.2 | async-start | bytes 2097152 | tf_op jit(solution)/shard_map/all_to_all | solution.py:243
  119.1 1.1 copy.30
  120.2 1.5 reshape.208.q_ref
  121.7 8.7 %shard_map.59 = bf16[2,256,1024]{2,1,0:T(8,128)(2,1)} custom-call(s32[2,6]{1,0:T(2,128)S(1)} %stack.4.chosen, s32[2,6]{1,0:T(2,128)S(1)} %stack.5.limits, bf16[2,256,1024]{2,1,0:T(8,128)(2,1)S(1)} %reshape.208.q_ref, bf16[2,2,256,128]{3,2,1,0:T(8,128)(2,1)S(1)} %bitcast.78, bf16[2,2,256,128]{3,2,1,0:T(8,128)(2,1)S(1)} %bitcast.79, ...), custom_call_target="tpu_custom_call" | custom-call | tf_op jit(solution)/shard_map/pallas_call | solution.py:198
  130.5 1.4 all-to-all-done.2
  131.9 3.6 %all-to-all-start.3 = ((bf16[2,256,1024]{2,1,0:T(8,128)(2,1)}), bf16[2,256,1024]{2,1,0:T(8,128)(2,1)S(1)}, u32[]{:S(2)}, u32[]{:S(2)}) async-start(bf16[2,256,1024]{2,1,0:T(8,128)(2,1)} %shard_map.59), calls=%async_computation.3 | async-start | bytes 2097152 | tf_op jit(solution)/shard_map/all_to_all | solution.py:243
  135.5 0.8 fusion.7
  136.3 0.8 fusion.6
  137.1 1.9 %fusion.5 = bf16[256,8192]{1,0:T(8,128)(2,1)} fusion(bf16[256,8192]{1,0:T(8,128)(2,1)} %fusion.6, bf16[2,256,1024]{2,1,0:T(8,128)(2,1)} %all-to-all-done.2), kind=kLoop, calls=%fused_computation.11 | loop fusion | bytes 1048576
  139.0 8.2 %all-to-all-done.3 = bf16[2,256,1024]{2,1,0:T(8,128)(2,1)S(1)} async-done(((bf16[2,256,1024]{2,1,0:T(8,128)(2,1)}), bf16[2,256,1024]{2,1,0:T(8,128)(2,1)S(1)}, u32[]{:S(2)}, u32[]{:S(2)}) %all-to-all-start.3) | async-done | bytes 1048608 | tf_op jit(solution)/shard_map/all_to_all | solution.py:243
  147.2 0.8 fusion.4
  148.1 0.8 fusion.3
  148.9 0.8 fusion.2
  149.7 1.9 %fusion.1 = bf16[256,8192]{1,0:T(8,128)(2,1)} fusion(bf16[256,8192]{1,0:T(8,128)(2,1)} %fusion.2, bf16[2,256,1024]{2,1,0:T(8,128)(2,1)} %all-to-all-done.2), kind=kLoop, calls=%fused_computation.3 | loop fusion | bytes 1048576
  151.6 0.8 fusion
  (32 shorter events, 3.3 us)
Async XLA Ops:
  5.2 5.2 %copy-start = (bf16[2,256,32,128]{3,2,1,0:T(8,128)(2,1)S(1)}, bf16[2,256,32,128]{3,2,1,0:T(8,128)(2,1)}, u32[]{:S(2)}) copy-start(bf16[2,256,32,128]{3,2,1,0:T(8,128)(2,1)} %param.5) | copy-start | bytes 12582916
  79.5 18.0 %all-to-all-start = ((bf16[2,256,1024]{2,1,0:T(8,128)(2,1)}), bf16[2,256,1024]{2,1,0:T(8,128)(2,1)S(1)}, u32[]{:S(2)}, u32[]{:S(2)}) async-start(bf16[2,256,1024]{2,1,0:T(8,128)(2,1)} %shard_map.56), calls=%async_computation | async-start | bytes 2097152 | tf_op jit(solution)/shard_map/all_to_all | solution.py:243
  97.5 17.2 %all-to-all-start.1 = ((bf16[2,256,1024]{2,1,0:T(8,128)(2,1)}), bf16[2,256,1024]{2,1,0:T(8,128)(2,1)S(1)}, u32[]{:S(2)}, u32[]{:S(2)}) async-start(bf16[2,256,1024]{2,1,0:T(8,128)(2,1)} %shard_map.57), calls=%async_computation.1 | async-start | bytes 2097152 | tf_op jit(solution)/shard_map/all_to_all | solution.py:243
  114.7 17.2 %all-to-all-start.2 = ((bf16[2,256,1024]{2,1,0:T(8,128)(2,1)}), bf16[2,256,1024]{2,1,0:T(8,128)(2,1)}, u32[]{:S(2)}, u32[]{:S(2)}) async-start(bf16[2,256,1024]{2,1,0:T(8,128)(2,1)} %shard_map.58), calls=%async_computation.2 | async-start | bytes 2097152 | tf_op jit(solution)/shard_map/all_to_all | solution.py:243
  131.9 15.3 %all-to-all-start.3 = ((bf16[2,256,1024]{2,1,0:T(8,128)(2,1)}), bf16[2,256,1024]{2,1,0:T(8,128)(2,1)S(1)}, u32[]{:S(2)}, u32[]{:S(2)}) async-start(bf16[2,256,1024]{2,1,0:T(8,128)(2,1)} %shard_map.59), calls=%async_computation.3 | async-start | bytes 2097152 | tf_op jit(solution)/shard_map/all_to_all | solution.py:243

commit v4 on v3

--- a/solution.py
+++ b/solution.py
@@ -13,16 +13,15 @@
 MESH = pl.DeviceIdType.MESH
 
 
-def attend(chosen, limits, q_ref, fk_ref, fv_ref, *rest):
+def attend(chosen, limits, where, q_ref, fk_ref, fv_ref, *rest):
     k_refs, v_refs, out_ref = rest[:PATH], rest[PATH : 2 * PATH], rest[2 * PATH]
-    r = pl.program_id(0)
-    tokens, width = q_ref.shape[1], fk_ref.shape[-1]
+    tokens, width = q_ref.shape[0], fk_ref.shape[-1]
     slots = k_refs[0].shape[-2]
-    group = q_ref.shape[2] // width
+    group = q_ref.shape[1] // width
     scale = math.log2(math.e) / math.sqrt(width)
 
     row = lax.broadcasted_iota(jnp.int32, (slots, width), 0)
-    marks = [jnp.where(row < limits[r, j], 0.0, MASKED).astype(jnp.bfloat16) for j in range(PATH)]
+    marks = [jnp.where(row < limits[j], 0.0, MASKED).astype(jnp.bfloat16) for j in range(PATH)]
     keys = jnp.concatenate([k[0, 0, 0, 0] for k in k_refs] + [fk_ref[0, 0]], axis=0)
     marks = jnp.concatenate(marks + [jnp.zeros((tokens, width), jnp.bfloat16)], axis=0)
     keys = jnp.concatenate([keys, marks], axis=1)
@@ -35,7 +34,7 @@
     past = PATH * slots
     for g in range(group):
         cols = slice(g * width, (g + 1) * width)
-        q = jnp.concatenate([q_ref[0, :, cols], first], axis=1)
+        q = jnp.concatenate([q_ref[:, cols], first], axis=1)
         scores = lax.dot_general(
             q, keys, (((1,), (1,)), ((), ())), preferred_element_type=jnp.float32
         )
@@ -44,7 +43,7 @@
         peak = jnp.max(scores, axis=1, keepdims=True)
         weights = jnp.exp2((scores - peak) * scale).astype(jnp.bfloat16)
         both = jnp.dot(weights, values, preferred_element_type=jnp.float32)
-        out_ref[0, :, cols] = (both[:, :width] / both[:, width:]).astype(jnp.bfloat16)
+        out_ref[:, cols] = (both[:, :width] / both[:, width:]).astype(jnp.bfloat16)
 
 
 def gather_kernel(columns, src, out, up_sem, down_sem, x_sem, near_sem, far_sem, recv_sem, own_sem):
@@ -180,38 +179,66 @@
     )(prefix)
 
 
-def attention(queries, fresh, prefix, chosen, limits, head):
-    requests, tokens, wide = queries.shape
-    blocks_dev = prefix.shape[2]
-    slots, width = prefix.shape[-2:]
+def attention(queries, fresh, prefix, chosen, limits, where, first, count, out_heads):
+    tokens = queries.shape[0]
+    blocks_dev, local_kv, slots, width = prefix.shape[2:]
+    wide = queries.shape[1] // local_kv
 
     def block_map(kv, j):
-        def place(r, chosen, limits):
-            return (chosen[r, j] // blocks_dev, kv, chosen[r, j] % blocks_dev, head, 0, 0)
+        def place(k, chosen, limits, where):
+            block = chosen[j]
+            return (block // blocks_dev, kv, block % blocks_dev, first + k, 0, 0)
 
         return place
 
     def fresh_map(kv):
-        return lambda r, chosen, limits: (kv, r, 0, 0)
-
-    q_spec = pl.BlockSpec((1, tokens, wide), lambda r, chosen, limits: (r, 0, 0))
+        return lambda k, chosen, limits, where: (kv, where[0], 0, first + k)
+
+    keys = PATH * slots + tokens
     return pl.pallas_call(
         attend,
-        out_shape=jax.ShapeDtypeStruct(queries.shape, jnp.bfloat16),
+        out_shape=jax.ShapeDtypeStruct((tokens, out_heads * wide), jnp.bfloat16),
         grid_spec=pltpu.PrefetchScalarGridSpec(
-            num_scalar_prefetch=2,
-            grid=(requests,),
-            in_specs=[q_spec]
+            num_scalar_prefetch=3,
+            grid=(count,),
+            in_specs=[pl.BlockSpec((tokens, wide), lambda k, chosen, limits, where: (0, first + k))]
             + [pl.BlockSpec((1, 1, tokens, width), fresh_map(kv)) for kv in (0, 1)]
             + [
                 pl.BlockSpec((1, 1, 1, 1, slots, width), block_map(kv, j))
                 for kv in (0, 1)
                 for j in range(PATH)
             ],
-            out_specs=q_spec,
+            out_specs=pl.BlockSpec((tokens, wide), lambda k, chosen, limits, where: (0, where[1] + k)),
+        ),
+        cost_estimate=pl.CostEstimate(
+            flops=8 * count * tokens * wide * keys,
+            bytes_accessed=count * 4 * (tokens * wide + keys * width),
+            transcendentals=count * tokens * wide // width * keys,
         ),
         compiler_params=pltpu.CompilerParams(vmem_limit_bytes=48 << 20),
-    )(chosen, limits, queries, fresh, fresh, *([prefix] * (2 * PATH)))
+    )(chosen, limits, where, queries, fresh, fresh, *([prefix] * (2 * PATH)))
+
+
+def place_kernel(where, piece_ref, whole_ref, out_ref):
+    out_ref[...] = piece_ref[...]
+
+
+def place(whole, piece, where, wide):
+    tokens, columns = piece.shape
+    return pl.pallas_call(
+        place_kernel,
+        out_shape=jax.ShapeDtypeStruct(whole.shape, whole.dtype),
+        grid_spec=pltpu.PrefetchScalarGridSpec(
+            num_scalar_prefetch=1,
+            grid=(columns // wide,),
+            in_specs=[
+                pl.BlockSpec((tokens, wide), lambda k, where: (0, k)),
+                pl.BlockSpec(memory_space=pl.ANY),
+            ],
+            out_specs=pl.BlockSpec((tokens, wide), lambda k, where: (0, where[0] + k)),
+        ),
+        input_output_aliases={2: 0},
+    )(where, piece, whole)
 
 
 def per_device(queries, fresh_key_value, prefix_kv, block_mask, valid_tokens):
@@ -230,18 +257,47 @@
     chosen = jnp.stack(chosen, axis=1).astype(jnp.int32)
     limits = jnp.stack(limits, axis=1).astype(jnp.int32)
     local_kv = fresh_key_value.shape[3]
-    group = local_heads // local_kv
+    wide = local_heads // local_kv * head_size
     parts = lax.axis_size("head")
-    rows = requests * length // parts
     gathered = gather(prefix_kv)
-    pieces = []
-    for k in range(local_kv):
-        q = queries[:, :, k * group : (k + 1) * group].reshape(requests, length, group * head_size)
-        fresh = fresh_key_value[:, :, :, k]
-        context = attention(q, fresh, gathered, chosen, limits, k)
-        context = context.reshape(parts, rows, group * head_size)
-        pieces.append(lax.all_to_all(context, "head", split_axis=0, concat_axis=0))
-    return jnp.concatenate([piece[i] for i in range(parts) for piece in pieces], axis=1)
+    fresh = fresh_key_value.reshape(2, requests, length, local_kv * head_size)
+
+    def attend_request(query_rows, request, first, count, base, out_heads):
+        pick = functools.partial(lax.dynamic_index_in_dim, axis=0, keepdims=False)
+        where = jnp.stack([jnp.int32(request), jnp.int32(base)])
+        return attention(
+            query_rows, fresh, gathered, pick(chosen, request), pick(limits, request), where, first, count, out_heads
+        )
+
+    def flat_queries(source, request):
+        rows = lax.dynamic_index_in_dim(source, request, axis=0, keepdims=False)
+        return rows.reshape(length, local_heads * head_size)
+
+    if parts != 2 or requests != 2:
+        context = jnp.concatenate(
+            [attend_request(flat_queries(queries, r), r, 0, local_kv, 0, local_kv) for r in range(requests)]
+        )
+        context = context.reshape(parts, requests * length // parts, local_kv * wide)
+        swapped = lax.all_to_all(context, "head", split_axis=0, concat_axis=0)
+        return jnp.concatenate([swapped[i] for i in range(parts)], axis=1)
+
+    mine = lax.axis_index("head")
+    other = 1 - mine
+    theirs = flat_queries(queries, other)
+    cuts = sorted({0, min(1, local_kv), min(2, local_kv), local_kv})
+    arrived = []
+    source = queries
+    for start, end in zip(cuts[:-1], cuts[1:]):
+        piece = attend_request(theirs, other, start, end - start, 0, end - start)
+        if start == 0:
+            source, piece = lax.optimization_barrier((source, piece))
+        arrived.append((start, lax.ppermute(piece, "head", [(0, 1), (1, 0)])))
+    whole = attend_request(
+        flat_queries(source, mine), mine, 0, local_kv, mine * local_kv, parts * local_kv
+    )
+    for start, piece in arrived:
+        whole = place(whole, piece, jnp.stack([other * local_kv + start]), wide)
+    return whole
 
 
 def solution(mesh):

time: 154 us -> 124 us (0.81)
  local copies, waits for them, and re-layouts: 25.6 us -> 9.68 us
  starting transfers between devices: 15.4 us -> 3.15 us
  waiting for transfers between devices: 15.8 us -> 9.06 us
  Pallas kernels: 91.4 us -> 96.7 us
    all_to_all x4 -> x0, waiting for transfers between devices: 15.8 us -> none  [per_device(): pieces.append(lax.all_to_all(context, 'head', split_axis=0, concat_axis=0))]
    all_to_all x4 -> x0, starting transfers between devices: 15.4 us -> none  [per_device(): pieces.append(lax.all_to_all(context, 'head', split_axis=0, concat_axis=0))]
    ppermute x0 -> x3, waiting for transfers between devices: none -> 9.06 us  [per_device(): arrived.append((start, lax.ppermute(piece, 'head', [(0, 1), (1, 0)])))]
    unnamed x13 -> x4, local copies, waits for them, and re-layouts: 11.1 us -> 2.97 us
    slice x2 -> x0, local copies, waits for them, and re-layouts: 7.31 us -> none  [the longest x1 5.17 us: per_device(): fresh = fresh_key_value[:, :, :, k]]
    pallas_call x4 -> x7, Pallas kernels: 34.8 us -> 40.1 us  [the longest x4 34.3 us: attention(): pl.pallas_call(attend, out_shape=jax.ShapeDtypeStruct((tokens, out_heads...]
    dynamic_slice x0 -> x2, local copies, waits for them, and re-layouts: none -> 3.91 us  [flat_queries(): rows = lax.dynamic_index_in_dim(source, request, axis=0, keepdims=False)]
    reshape x4 -> x1, local copies, waits for them, and re-layouts: 5.05 us -> 1.47 us  [per_device(): fresh = fresh_key_value.reshape(2, requests, length, local_kv * head_size)]
  transfers between devices with their start and end apart: 4 -> 3, of which waited for: 4 -> 1; matrix products, arithmetic and copies ran while one was open for 7% -> 2% of each run, Pallas kernels for 17% -> 27%
where the time goes in v4:
time: 124 us; the launch traced here: 123 us
  Pallas kernels  96.7 us (78%)
  local copies, waits for them, and re-layouts  9.68 us (8%)
  waiting for transfers between devices  9.06 us (7%)
  other arithmetic  4.21 us (3%)
  starting transfers between devices  3.15 us (3%)
    pallas_call x1, Pallas kernels, gather(): pl.pallas_call(functools.partial(gather_kernel, columns), out_shape=jax.S...  56.6 us
    pallas_call x4, Pallas kernels, attention(): pl.pallas_call(attend, out_shape=jax.ShapeDtypeStruct((tokens, out_heads...  34.3 us
    ppermute x3, waiting for transfers between devices, per_device(): arrived.append((start, lax.ppermute(piece, 'head', [(0, 1), (1, 0)])))  9.06 us
    pallas_call x3, Pallas kernels, place(): pl.pallas_call(place_kernel, out_shape=jax.ShapeDtypeStruct(whole.shape,...  5.78 us
    dynamic_slice x2, local copies, waits for them, and re-layouts, flat_queries(): rows = lax.dynamic_index_in_dim(source, request, axis=0, keepdims=False)  3.91 us
    ppermute x3, starting transfers between devices, per_device(): arrived.append((start, lax.ppermute(piece, 'head', [(0, 1), (1, 0)])))  3.15 us
    reduce_max x6, other arithmetic, per_device(): best = jnp.max(ranking, axis=1)  3.09 us
    unnamed x4, local copies, waits for them, and re-layouts  2.97 us
  transfers between devices with their start and end apart: 3, of which 1 were waited for; matrix products, arithmetic and copies ran while one was open for 2% of the time, Pallas kernels for 27%

profile of v4, /device:TPU:0, one launch (start us, length us, event | category | flops | bytes accessed | tf_op | source)
XLA Modules:
  0.0 122.8 jit_solution(548127509902339876)
XLA Ops:
  0.0 0.8 fusion.17
  0.8 0.9 fusion.5
  1.7 0.9 fusion.26
  2.6 0.2 fusion.6
  2.8 0.2 fusion.24
  2.9 0.2 select_reduce_fusion.5
  3.2 0.9 fusion
  4.2 0.1 copy.16
  4.3 0.1 copy.17
  4.4 0.1 copy.18
  4.5 0.1 copy.19
  4.6 0.1 copy.15
  5.3 0.1 stack.22
  5.4 0.1 stack.21
  5.5 1.5 %reshape.205.fk_ref.fv_ref = bf16[2,2,256,512]{3,2,1,0:T(8,128)(2,1)S(1)} reshape(bf16[2,2,256,4,128]{4,3,2,1,0:T(4,128)(2,1)} %param.6) | data formatting | bytes 2097152 | tf_op jit(solution)/shard_map/reshape | solution.py:263
  7.0 2.0 %constant_dynamic-slice_fusion.3 = bf16[1,256,32,128]{3,2,1,0:T(8,128)(2,1)S(1)} fusion(bf16[2,256,32,128]{3,2,1,0:T(8,128)(2,1)} %param.5, s32[]{:T(128)S(6)} %select_n.236), kind=kLoop, calls=%fused_computation.7 | loop fusion | bytes 4194308 | tf_op jit(solution)/shard_map/jit(dynamic_index_in_dim)/dynamic_slice | solution.py:273
  8.9 1.0 copy.26
  9.9 56.6 %shard_map.55.rest_0_.rest_1_.rest_2_.rest_3_.rest_4_.rest_5_.rest_6_.rest_7_.rest_8_.rest_9_.rest_10_.rest_11_ = bf16[16,2,2,4,128,128]{5,4,3,2,1,0:T(8,128)(2,1)} custom-call(bf16[2,2,4,128,128]{4,3,2,1,0:T(8,128)(2,1)} %src.1), custom_call_target="tpu_custom_call" | custom-call | tf_op jit(solution)/shard_map/pallas_call | solution.py:172
  66.5 5.3 %shard_map.57 = bf16[256,1024]{1,0:T(8,128)(2,1)} custom-call(s32[6]{0:T(128)S(1)} %get-tuple-element.22.chosen, s32[6]{0:T(128)S(1)} %get-tuple-element.20.limits, s32[2]{0:T(128)S(1)} %get-tuple-element.36.where, bf16[256,4096]{1,0:T(8,128)(2,1)S(1)} %bitcast.48, bf16[2,2,256,512]{3,2,1,0:T(8,128)(2,1)S(1)} %reshape.205.fk_ref.fv_ref, ...), custom_call_target="tpu_custom_call" | custom-call | flops 2147483648 | bytes 1572864 | tf_op jit(solution)/shard_map/pallas_call | solution.py:198
  71.8 1.5 %collective-permute-start.1 = (bf16[256,1024]{1,0:T(8,128)(2,1)}, bf16[256,1024]{1,0:T(8,128)(2,1)}, u32[]{:S(2)}, u32[]{:S(2)}) collective-permute-start(bf16[256,1024]{1,0:T(8,128)(2,1)} %shard_map.57), channel_id=1, source_target_pairs={{0,1},{1,0},{2,3},{3,2},{4,5},{5,4},{6,7},{7,6},{8,9},{9,8},{10,11... | collective-permute-start | bytes 1572872 | tf_op jit(solution)/shard_map/ppermute | solution.py:294
  73.2 5.3 %shard_map.58 = bf16[256,1024]{1,0:T(8,128)(2,1)} custom-call(s32[6]{0:T(128)S(1)} %get-tuple-element.22.chosen, s32[6]{0:T(128)S(1)} %get-tuple-element.20.limits, s32[2]{0:T(128)S(1)} %get-tuple-element.36.where, bf16[256,4096]{1,0:T(8,128)(2,1)S(1)} %bitcast.49, bf16[2,2,256,512]{3,2,1,0:T(8,128)(2,1)S(1)} %reshape.205.fk_ref.fv_ref, ...), custom_call_target="tpu_custom_call" | custom-call | flops 2147483648 | bytes 1572864 | tf_op jit(solution)/shard_map/pallas_call | solution.py:198
  78.5 0.5 collective-permute-start.2
  79.0 9.0 %shard_map.56 = bf16[256,2048]{1,0:T(8,128)(2,1)} custom-call(s32[6]{0:T(128)S(1)} %get-tuple-element.22.chosen, s32[6]{0:T(128)S(1)} %get-tuple-element.20.limits, s32[2]{0:T(128)S(1)} %get-tuple-element.36.where, bf16[256,4096]{1,0:T(8,128)(2,1)S(1)} %bitcast.50, bf16[2,2,256,512]{3,2,1,0:T(8,128)(2,1)S(1)} %reshape.205.fk_ref.fv_ref, ...), custom_call_target="tpu_custom_call" | custom-call | flops 4294967296 | bytes 3145728 | tf_op jit(solution)/shard_map/pallas_call | solution.py:198
  88.0 1.2 collective-permute-start
  89.2 2.0 %constant_dynamic-slice_fusion = bf16[1,256,32,128]{3,2,1,0:T(8,128)(2,1)S(1)} fusion(bf16[2,256,32,128]{3,2,1,0:T(8,128)(2,1)} %param.5, s32[]{:T(128)S(6)} %select_n.255), kind=kLoop, calls=%fused_computation.4 | loop fusion | bytes 4194308 | tf_op jit(solution)/shard_map/jit(dynamic_index_in_dim)/dynamic_slice | solution.py:273
  91.2 1.0 copy.25
  92.3 14.8 %shard_map.59.whole_ref = bf16[256,8192]{1,0:T(8,128)(2,1)} custom-call(s32[6]{0:T(128)S(1)} %get-tuple-element.21.chosen, s32[6]{0:T(128)S(1)} %get-tuple-element.19.limits, s32[2]{0:T(128)S(1)} %pad_add_fusion.1.where, bf16[256,4096]{1,0:T(8,128)(2,1)S(1)} %bitcast.51, bf16[2,2,256,512]{3,2,1,0:T(8,128)(2,1)S(1)} %reshape.205.fk_ref.fv_ref, ...), custom_call_target="tpu_custom_call" | custom-call | flops 8589934592 | bytes 6291456 | tf_op jit(solution)/shard_map/pallas_call | solution.py:198
  107.0 1.9 %shard_map.60.whole_ref = bf16[256,8192]{1,0:T(8,128)(2,1)} custom-call(s32[1]{0:T(128)} %bitcast.17.where, bf16[256,1024]{1,0:T(8,128)(2,1)} %collective-permute-done.2.piece_ref, bf16[256,8192]{1,0:T(8,128)(2,1)} %shard_map.59.whole_ref), custom_call_target="tpu_custom_call", output_to_operand_aliasing={{}: (2, {})} | custom-call | tf_op jit(solution)/shard_map/pallas_call | solution.py:228
  108.9 1.9 %shard_map.61.whole_ref = bf16[256,8192]{1,0:T(8,128)(2,1)} custom-call(s32[1]{0:T(128)} %bitcast.16.where, bf16[256,1024]{1,0:T(8,128)(2,1)} %collective-permute-done.1.piece_ref, bf16[256,8192]{1,0:T(8,128)(2,1)} %shard_map.60.whole_ref), custom_call_target="tpu_custom_call", output_to_operand_aliasing={{}: (2, {})} | custom-call | tf_op jit(solution)/shard_map/pallas_call | solution.py:228
  110.8 9.1 %collective-permute-done.piece_ref = bf16[256,2048]{1,0:T(8,128)(2,1)S(1)} collective-permute-done((bf16[256,2048]{1,0:T(8,128)(2,1)}, bf16[256,2048]{1,0:T(8,128)(2,1)S(1)}, u32[]{:S(2)}, u32[]{:S(2)}) %collective-permute-start) | collective-permute-done | bytes 1048608 | tf_op jit(solution)/shard_map/ppermute | solution.py:294
  119.8 1.0 copy-done
  120.8 2.0 %shard_map.62 = bf16[256,8192]{1,0:T(8,128)(2,1)} custom-call(s32[1]{0:T(128)} %bitcast.where, bf16[256,2048]{1,0:T(8,128)(2,1)} %copy-done, bf16[256,8192]{1,0:T(8,128)(2,1)} %shard_map.61.whole_ref), custom_call_target="tpu_custom_call", output_to_operand_aliasing={{}: (2, {})} | custom-call | tf_op jit(solution)/shard_map/pallas_call | solution.py:228
  (26 shorter events, 0.9 us)
Async XLA Ops:
  71.8 37.1 %collective-permute-start.1 = (bf16[256,1024]{1,0:T(8,128)(2,1)}, bf16[256,1024]{1,0:T(8,128)(2,1)}, u32[]{:S(2)}, u32[]{:S(2)}) collective-permute-start(bf16[256,1024]{1,0:T(8,128)(2,1)} %shard_map.57), channel_id=1, source_target_pairs={{0,1},{1,0},{2,3},{3,2},{4,5},{5,4},{6,7},{7,6},{8,9},{9,8},{10,11... | collective-permute-start | bytes 1572872 | tf_op jit(solution)/shard_map/ppermute | solution.py:294
  78.5 28.5 %collective-permute-start.2 = (bf16[256,1024]{1,0:T(8,128)(2,1)}, bf16[256,1024]{1,0:T(8,128)(2,1)}, u32[]{:S(2)}, u32[]{:S(2)}) collective-permute-start(bf16[256,1024]{1,0:T(8,128)(2,1)} %shard_map.58), channel_id=1, source_target_pairs={{0,1},{1,0},{2,3},{3,2},{4,5},{5,4},{6,7},{7,6},{8,9},{9,8},{10,11... | collective-permute-start | bytes 1572872 | tf_op jit(solution)/shard_map/ppermute | solution.py:294
  88.0 31.8 %collective-permute-start = (bf16[256,2048]{1,0:T(8,128)(2,1)}, bf16[256,2048]{1,0:T(8,128)(2,1)S(1)}, u32[]{:S(2)}, u32[]{:S(2)}) collective-permute-start(bf16[256,2048]{1,0:T(8,128)(2,1)} %shard_map.56), channel_id=1, source_target_pairs={{0,1},{1,0},{2,3},{3,2},{4,5},{5,4},{6,7},{7,6},{8,9},{9,8},{10,11... | collective-permute-start | bytes 3145736 | tf_op jit(solution)/shard_map/ppermute | solution.py:294
  119.8 1.0 copy-start

commit v5 on v4

--- a/solution.py
+++ b/solution.py
@@ -46,10 +46,11 @@
         out_ref[:, cols] = (both[:, :width] / both[:, width:]).astype(jnp.bfloat16)
 
 
-def gather_kernel(columns, src, out, up_sem, down_sem, x_sem, near_sem, far_sem, recv_sem, own_sem):
+def gather_kernel(columns, low, high, src, out, up_sem, down_sem, x_sem, near_sem, far_sem, recv_sem, own_sem):
     me = lax.axis_index("req")
     core, x, z = me % 2, (me // 2) % 2, me // 4
     last = columns - 1
+    own_part = src.at[:, :, low:high]
 
     def at(z_at, x_at, core_at):
         return z_at * 4 + x_at * 2 + core_at
@@ -75,7 +76,7 @@
 
     def copy(shard, send_sem, device, from_src=False):
         return pltpu.make_async_remote_copy(
-            src_ref=src if from_src else out.at[shard],
+            src_ref=own_part if from_src else out.at[shard],
             dst_ref=out.at[shard],
             send_sem=send_sem,
             recv_sem=recv_sem.at[shard],
@@ -138,7 +139,7 @@
             arrived(shard)
             send.start()
 
-    keep = pltpu.make_async_copy(src, out.at[me], own_sem)
+    keep = pltpu.make_async_copy(own_part, out.at[me], own_sem)
     step_column(column[0])
     keep.start()
     for d in range(1, columns):
@@ -164,30 +165,35 @@
     keep.wait()
 
 
-def gather(prefix):
+def gather(prefix, low, high, collective):
     devices = lax.axis_size("req")
     columns = devices // 4
     slots = 2 * columns - 1
     dma = pltpu.SemaphoreType.DMA
     return pl.pallas_call(
-        functools.partial(gather_kernel, columns),
-        out_shape=jax.ShapeDtypeStruct((devices,) + prefix.shape, prefix.dtype),
+        functools.partial(gather_kernel, columns, low, high),
+        out_shape=jax.ShapeDtypeStruct(
+            (devices,) + prefix.shape[:2] + (high - low,) + prefix.shape[3:], prefix.dtype
+        ),
         in_specs=[pl.BlockSpec(memory_space=pl.ANY)],
         out_specs=pl.BlockSpec(memory_space=pl.ANY),
         scratch_shapes=[dma((slots,))] * 5 + [dma((devices,)), dma],
-        compiler_params=pltpu.CompilerParams(collective_id=1, has_side_effects=True),
+        cost_estimate=pl.CostEstimate(
+            flops=0, bytes_accessed=16 * devices * prefix.size * (high - low) // prefix.shape[2], transcendentals=0
+        ),
+        compiler_params=pltpu.CompilerParams(collective_id=collective, has_side_effects=True),
     )(prefix)
 
 
-def attention(queries, fresh, prefix, chosen, limits, where, first, count, out_heads):
+def attention(queries, fresh, prefix, chosen, limits, where, first, count, out_heads, low):
     tokens = queries.shape[0]
-    blocks_dev, local_kv, slots, width = prefix.shape[2:]
-    wide = queries.shape[1] // local_kv
+    blocks_dev, _, slots, width = prefix.shape[2:]
+    wide = queries.shape[1] // (fresh.shape[-1] // width)
 
     def block_map(kv, j):
         def place(k, chosen, limits, where):
             block = chosen[j]
-            return (block // blocks_dev, kv, block % blocks_dev, first + k, 0, 0)
+            return (block // blocks_dev, kv, block % blocks_dev, first - low + k, 0, 0)
 
         return place
 
@@ -259,14 +265,13 @@
     local_kv = fresh_key_value.shape[3]
     wide = local_heads // local_kv * head_size
     parts = lax.axis_size("head")
-    gathered = gather(prefix_kv)
     fresh = fresh_key_value.reshape(2, requests, length, local_kv * head_size)
 
-    def attend_request(query_rows, request, first, count, base, out_heads):
+    def attend_request(query_rows, gathered, low, request, first, count, base, out_heads):
         pick = functools.partial(lax.dynamic_index_in_dim, axis=0, keepdims=False)
         where = jnp.stack([jnp.int32(request), jnp.int32(base)])
         return attention(
-            query_rows, fresh, gathered, pick(chosen, request), pick(limits, request), where, first, count, out_heads
+            query_rows, fresh, gathered, pick(chosen, request), pick(limits, request), where, first, count, out_heads, low
         )
 
     def flat_queries(source, request):
@@ -274,8 +279,9 @@
         return rows.reshape(length, local_heads * head_size)
 
     if parts != 2 or requests != 2:
+        gathered = gather(prefix_kv, 0, local_kv, 1)
         context = jnp.concatenate(
-            [attend_request(flat_queries(queries, r), r, 0, local_kv, 0, local_kv) for r in range(requests)]
+            [attend_request(flat_queries(queries, r), gathered, 0, r, 0, local_kv, 0, local_kv) for r in range(requests)]
         )
         context = context.reshape(parts, requests * length // parts, local_kv * wide)
         swapped = lax.all_to_all(context, "head", split_axis=0, concat_axis=0)
@@ -284,17 +290,28 @@
     mine = lax.axis_index("head")
     other = 1 - mine
     theirs = flat_queries(queries, other)
-    cuts = sorted({0, min(1, local_kv), min(2, local_kv), local_kv})
-    arrived = []
-    source = queries
-    for start, end in zip(cuts[:-1], cuts[1:]):
-        piece = attend_request(theirs, other, start, end - start, 0, end - start)
-        if start == 0:
+    half = max(local_kv // 2, 1)
+    arrived, held, source, prefix = [], [], queries, prefix_kv
+    for low in range(0, local_kv, half):
+        high = min(low + half, local_kv)
+        gathered = gather(prefix, low, high, 1 + low // half)
+        held.append((low, high, gathered))
+        step = half if high < local_kv else 1
+        for start in range(low, high, step):
+            count = min(step, high - start)
+            piece = attend_request(theirs, gathered, low, other, start, count, 0, count)
+            if high < local_kv:
+                prefix, piece = lax.optimization_barrier((prefix, piece))
             source, piece = lax.optimization_barrier((source, piece))
-        arrived.append((start, lax.ppermute(piece, "head", [(0, 1), (1, 0)])))
+            arrived.append((start, lax.ppermute(piece, "head", [(0, 1), (1, 0)])))
+    own_rows = flat_queries(source, mine)
+    low, high, gathered = held[0]
     whole = attend_request(
-        flat_queries(source, mine), mine, 0, local_kv, mine * local_kv, parts * local_kv
+        own_rows, gathered, low, mine, low, high - low, mine * local_kv, parts * local_kv
     )
+    for low, high, gathered in held[1:]:
+        piece = attend_request(own_rows, gathered, low, mine, low, high - low, 0, high - low)
+        whole = place(whole, piece, jnp.stack([mine * local_kv + low]), wide)
     for start, piece in arrived:
         whole = place(whole, piece, jnp.stack([other * local_kv + start]), wide)
     return whole

time: 124 us -> 125 us (level)
  Pallas kernels: 96.7 us -> 107 us
  waiting for transfers between devices: 9.06 us -> 0.86 us
  local copies, waits for them, and re-layouts: 9.68 us -> 8.07 us
    ppermute x3, waiting for transfers between devices: 9.06 us -> 0.86 us  [per_device(): arrived.append((start, lax.ppermute(piece, 'head', [(0, 1), (1, 0)])))]
    pallas_call x1 -> x2, Pallas kernels: 56.6 us -> 63.7 us  [gather(): pl.pallas_call(functools.partial(gather_kernel, columns, low, high), out_...]
    pallas_call x3 -> x4, Pallas kernels: 5.78 us -> 7.84 us  [place(): pl.pallas_call(place_kernel, out_shape=jax.ShapeDtypeStruct(whole.shape,...]
    dynamic_slice x2, local copies, waits for them, and re-layouts: 3.91 us -> 2.32 us  [flat_queries(): rows = lax.dynamic_index_in_dim(source, request, axis=0, keepdims=False)]
    pallas_call x4 -> x5, Pallas kernels: 34.3 us -> 35.9 us  [attention(): pl.pallas_call(attend, out_shape=jax.ShapeDtypeStruct((tokens, out_heads...]
    unnamed x4 -> x6, local copies, waits for them, and re-layouts: 2.97 us -> 2.95 us
  transfers between devices with their start and end apart: 3 -> 3, of which waited for: 1 -> 1; matrix products, arithmetic and copies ran while one was open for 2% -> 1% of each run, Pallas kernels for 27% -> 51%
where the time goes in v5:
time: 125 us; the launch traced here: 124 us
  Pallas kernels  107 us (86%)
  local copies, waits for them, and re-layouts  8.07 us (6%)
  other arithmetic  4.21 us (3%)
  starting transfers between devices  3.27 us (3%)
    pallas_call x2, Pallas kernels, gather(): pl.pallas_call(functools.partial(gather_kernel, columns, low, high), out_...  63.7 us
    pallas_call x5, Pallas kernels, attention(): pl.pallas_call(attend, out_shape=jax.ShapeDtypeStruct((tokens, out_heads...  35.9 us
    pallas_call x4, Pallas kernels, place(): pl.pallas_call(place_kernel, out_shape=jax.ShapeDtypeStruct(whole.shape,...  7.84 us
    ppermute x3, starting transfers between devices, per_device(): arrived.append((start, lax.ppermute(piece, 'head', [(0, 1), (1, 0)])))  3.27 us
    reduce_max x6, other arithmetic, per_device(): best = jnp.max(ranking, axis=1)  3.09 us
    unnamed x6, local copies, waits for them, and re-layouts  2.95 us
  transfers between devices with their start and end apart: 3, of which 1 were waited for; matrix products, arithmetic and copies ran while one was open for 1% of the time, Pallas kernels for 51%

profile of v5, /device:TPU:0, one launch (start us, length us, event | category | flops | bytes accessed | tf_op | source)
XLA Modules:
  0.0 124.0 jit_solution(2302131072080810502)
XLA Ops:
  0.0 0.8 fusion.17
  0.8 0.9 fusion.5
  1.7 0.9 fusion.26
  2.6 0.2 fusion.6
  2.8 0.2 fusion.24
  2.9 0.2 select_reduce_fusion.5
  3.2 0.9 fusion
  4.2 0.1 copy.17
  4.3 0.1 copy.18
  5.3 0.1 stack.26
  5.4 0.1 stack.25
  5.5 1.5 %reshape.205.fk_ref.fv_ref = bf16[2,2,256,512]{3,2,1,0:T(8,128)(2,1)S(1)} reshape(bf16[2,2,256,4,128]{4,3,2,1,0:T(4,128)(2,1)} %param.6) | data formatting | bytes 2097152 | tf_op jit(solution)/shard_map/reshape | solution.py:268
  7.0 2.0 %constant_dynamic-slice_fusion.3 = bf16[1,256,32,128]{3,2,1,0:T(8,128)(2,1)S(1)} fusion(bf16[2,256,32,128]{3,2,1,0:T(8,128)(2,1)} %param.5, s32[]{:T(128)S(6)} %select_n.238), kind=kLoop, calls=%fused_computation.7 | loop fusion | bytes 4194308 | tf_op jit(solution)/shard_map/jit(dynamic_index_in_dim)/dynamic_slice | solution.py:278
  8.9 1.0 copy.27
  9.9 33.7 %shard_map.55.rest_0_.rest_1_.rest_2_.rest_3_.rest_4_.rest_5_.rest_6_.rest_7_.rest_8_.rest_9_.rest_10_.rest_11_ = bf16[16,2,2,2,128,128]{5,4,3,2,1,0:T(8,128)(2,1)} custom-call(bf16[2,2,4,128,128]{4,3,2,1,0:T(8,128)(2,1)} %src.2), custom_call_target="tpu_custom_call" | custom-call | bytes 33554432 | tf_op jit(solution)/shard_map/pallas_call | solution.py:173
  43.7 8.8 %shard_map.56 = bf16[256,2048]{1,0:T(8,128)(2,1)} custom-call(s32[6]{0:T(128)S(1)} %get-tuple-element.34.chosen, s32[6]{0:T(128)S(1)} %get-tuple-element.32.limits, s32[2]{0:T(128)S(1)} %get-tuple-element.49.where, bf16[256,4096]{1,0:T(8,128)(2,1)S(1)} %bitcast.49, bf16[2,2,256,512]{3,2,1,0:T(8,128)(2,1)S(1)} %reshape.205.fk_ref.fv_ref, ...), custom_call_target="tpu_custom_call" | custom-call | flops 4294967296 | bytes 3145728 | tf_op jit(solution)/shard_map/pallas_call | solution.py:204
  52.5 1.2 %collective-permute-start.2 = (bf16[256,2048]{1,0:T(8,128)(2,1)}, bf16[256,2048]{1,0:T(8,128)(2,1)}, u32[]{:S(2)}, u32[]{:S(2)}) collective-permute-start(bf16[256,2048]{1,0:T(8,128)(2,1)} %shard_map.56), channel_id=1, source_target_pairs={{0,1},{1,0},{2,3},{3,2},{4,5},{5,4},{6,7},{7,6},{8,9},{9,8},{10,11... | collective-permute-start | bytes 3145736 | tf_op jit(solution)/shard_map/ppermute | solution.py:306
  53.8 30.0 %shard_map.57.rest_0_.rest_1_.rest_2_.rest_3_.rest_4_.rest_5_.rest_6_.rest_7_.rest_8_.rest_9_.rest_10_.rest_11_ = bf16[16,2,2,2,128,128]{5,4,3,2,1,0:T(8,128)(2,1)} custom-call(bf16[2,2,4,128,128]{4,3,2,1,0:T(8,128)(2,1)} %src.2), custom_call_target="tpu_custom_call" | custom-call | bytes 33554432 | tf_op jit(solution)/shard_map/pallas_call | solution.py:173
  83.8 5.3 %shard_map.59 = bf16[256,1024]{1,0:T(8,128)(2,1)} custom-call(s32[6]{0:T(128)S(1)} %get-tuple-element.34.chosen, s32[6]{0:T(128)S(1)} %get-tuple-element.32.limits, s32[2]{0:T(128)S(1)} %get-tuple-element.49.where, bf16[256,4096]{1,0:T(8,128)(2,1)S(1)} %bitcast.50, bf16[2,2,256,512]{3,2,1,0:T(8,128)(2,1)S(1)} %reshape.205.fk_ref.fv_ref, ...), custom_call_target="tpu_custom_call" | custom-call | flops 2147483648 | bytes 1572864 | tf_op jit(solution)/shard_map/pallas_call | solution.py:204
  89.1 5.4 %shard_map.58 = bf16[256,1024]{1,0:T(8,128)(2,1)} custom-call(s32[6]{0:T(128)S(1)} %get-tuple-element.34.chosen, s32[6]{0:T(128)S(1)} %get-tuple-element.32.limits, s32[2]{0:T(128)S(1)} %get-tuple-element.49.where, bf16[256,4096]{1,0:T(8,128)(2,1)S(1)} %bitcast.51, bf16[2,2,256,512]{3,2,1,0:T(8,128)(2,1)S(1)} %reshape.205.fk_ref.fv_ref, ...), custom_call_target="tpu_custom_call" | custom-call | flops 2147483648 | bytes 1572864 | tf_op jit(solution)/shard_map/pallas_call | solution.py:204
  94.5 0.4 collective-permute-start
  94.9 1.7 %collective-permute-start.1 = (bf16[256,1024]{1,0:T(8,128)(2,1)}, bf16[256,1024]{1,0:T(8,128)(2,1)}, u32[]{:S(2)}, u32[]{:S(2)}) collective-permute-start(bf16[256,1024]{1,0:T(8,128)(2,1)} %shard_map.58), channel_id=1, source_target_pairs={{0,1},{1,0},{2,3},{3,2},{4,5},{5,4},{6,7},{7,6},{8,9},{9,8},{10,11... | collective-permute-start | bytes 1572872 | tf_op jit(solution)/shard_map/ppermute | solution.py:306
  96.6 0.4 constant_dynamic-slice_fusion
  96.9 1.0 copy.26
  97.9 8.0 %shard_map.60.piece_ref = bf16[256,2048]{1,0:T(8,128)(2,1)S(1)} custom-call(s32[6]{0:T(128)S(1)} %get-tuple-element.33.chosen, s32[6]{0:T(128)S(1)} %get-tuple-element.31.limits, s32[2]{0:T(128)S(1)} %get-tuple-element.48.where, bf16[256,4096]{1,0:T(8,128)(2,1)S(1)} %bitcast.52, bf16[2,2,256,512]{3,2,1,0:T(8,128)(2,1)S(1)} %reshape.205.fk_ref.fv_ref, ...), custom_call_target="tpu_custom_call" | custom-call | flops 4294967296 | bytes 3145728 | tf_op jit(solution)/shard_map/pallas_call | solution.py:204
  105.9 1.0 copy-done
  106.9 8.4 %shard_map.61.whole_ref = bf16[256,8192]{1,0:T(8,128)(2,1)} custom-call(s32[6]{0:T(128)S(1)} %get-tuple-element.33.chosen, s32[6]{0:T(128)S(1)} %get-tuple-element.31.limits, s32[2]{0:T(128)S(1)} %get-tuple-element.50.where, bf16[256,4096]{1,0:T(8,128)(2,1)S(1)} %bitcast.53, bf16[2,2,256,512]{3,2,1,0:T(8,128)(2,1)S(1)} %reshape.205.fk_ref.fv_ref, ...), custom_call_target="tpu_custom_call" | custom-call | flops 4294967296 | bytes 3145728 | tf_op jit(solution)/shard_map/pallas_call | solution.py:204
  115.3 2.1 %shard_map.62.whole_ref = bf16[256,8192]{1,0:T(8,128)(2,1)} custom-call(s32[1]{0:T(128)} %bitcast.18.where, bf16[256,2048]{1,0:T(8,128)(2,1)} %copy-done, bf16[256,8192]{1,0:T(8,128)(2,1)} %shard_map.61.whole_ref), custom_call_target="tpu_custom_call", output_to_operand_aliasing={{}: (2, {})} | custom-call | tf_op jit(solution)/shard_map/pallas_call | solution.py:234
  117.3 2.0 %shard_map.63.whole_ref = bf16[256,8192]{1,0:T(8,128)(2,1)} custom-call(s32[1]{0:T(128)} %bitcast.17.where, bf16[256,2048]{1,0:T(8,128)(2,1)} %collective-permute-done.2.piece_ref, bf16[256,8192]{1,0:T(8,128)(2,1)} %shard_map.62.whole_ref), custom_call_target="tpu_custom_call", output_to_operand_aliasing={{}: (2, {})} | custom-call | tf_op jit(solution)/shard_map/pallas_call | solution.py:234
  119.4 0.9 collective-permute-done.1.piece_ref
  120.2 1.9 %shard_map.64.whole_ref = bf16[256,8192]{1,0:T(8,128)(2,1)} custom-call(s32[1]{0:T(128)} %bitcast.16.where, bf16[256,1024]{1,0:T(8,128)(2,1)} %collective-permute-done.1.piece_ref, bf16[256,8192]{1,0:T(8,128)(2,1)} %shard_map.63.whole_ref), custom_call_target="tpu_custom_call", output_to_operand_aliasing={{}: (2, {})} | custom-call | tf_op jit(solution)/shard_map/pallas_call | solution.py:234
  122.1 1.9 %shard_map.65 = bf16[256,8192]{1,0:T(8,128)(2,1)} custom-call(s32[1]{0:T(128)} %bitcast.where, bf16[256,1024]{1,0:T(8,128)(2,1)} %collective-permute-done.piece_ref, bf16[256,8192]{1,0:T(8,128)(2,1)} %shard_map.64.whole_ref), custom_call_target="tpu_custom_call", output_to_operand_aliasing={{}: (2, {})} | custom-call | tf_op jit(solution)/shard_map/pallas_call | solution.py:234
  (31 shorter events, 1.2 us)
Async XLA Ops:
  52.5 64.8 %collective-permute-start.2 = (bf16[256,2048]{1,0:T(8,128)(2,1)}, bf16[256,2048]{1,0:T(8,128)(2,1)}, u32[]{:S(2)}, u32[]{:S(2)}) collective-permute-start(bf16[256,2048]{1,0:T(8,128)(2,1)} %shard_map.56), channel_id=1, source_target_pairs={{0,1},{1,0},{2,3},{3,2},{4,5},{5,4},{6,7},{7,6},{8,9},{9,8},{10,11... | collective-permute-start | bytes 3145736 | tf_op jit(solution)/shard_map/ppermute | solution.py:306
  89.1 7.5 %copy-start.1 = (bf16[2,256,32,128]{3,2,1,0:T(8,128)(2,1)S(1)}, bf16[2,256,32,128]{3,2,1,0:T(8,128)(2,1)}, u32[]{:S(2)}) copy-start(bf16[2,256,32,128]{3,2,1,0:T(8,128)(2,1)} %param.5) | copy-start | bytes 12582916
  94.5 27.6 %collective-permute-start = (bf16[256,1024]{1,0:T(8,128)(2,1)}, bf16[256,1024]{1,0:T(8,128)(2,1)}, u32[]{:S(2)}, u32[]{:S(2)}) collective-permute-start(bf16[256,1024]{1,0:T(8,128)(2,1)} %shard_map.59), channel_id=1, source_target_pairs={{0,1},{1,0},{2,3},{3,2},{4,5},{5,4},{6,7},{7,6},{8,9},{9,8},{10,11... | collective-permute-start | bytes 1572872 | tf_op jit(solution)/shard_map/ppermute | solution.py:306
  94.9 25.3 %collective-permute-start.1 = (bf16[256,1024]{1,0:T(8,128)(2,1)}, bf16[256,1024]{1,0:T(8,128)(2,1)}, u32[]{:S(2)}, u32[]{:S(2)}) collective-permute-start(bf16[256,1024]{1,0:T(8,128)(2,1)} %shard_map.58), channel_id=1, source_target_pairs={{0,1},{1,0},{2,3},{3,2},{4,5},{5,4},{6,7},{7,6},{8,9},{9,8},{10,11... | collective-permute-start | bytes 1572872 | tf_op jit(solution)/shard_map/ppermute | solution.py:306
  105.9 1.0 copy-start

commit v6 on v5

--- a/solution.py
+++ b/solution.py
@@ -14,7 +14,7 @@
 
 
 def attend(chosen, limits, where, q_ref, fk_ref, fv_ref, *rest):
-    k_refs, v_refs, out_ref = rest[:PATH], rest[PATH : 2 * PATH], rest[2 * PATH]
+    k_refs, v_refs, out_ref = rest[:PATH], rest[PATH : 2 * PATH], rest[-1]
     tokens, width = q_ref.shape[0], fk_ref.shape[-1]
     slots = k_refs[0].shape[-2]
     group = q_ref.shape[1] // width
@@ -185,7 +185,7 @@
     )(prefix)
 
 
-def attention(queries, fresh, prefix, chosen, limits, where, first, count, out_heads, low):
+def attention(queries, fresh, prefix, chosen, limits, where, first, count, out_heads, low, into=()):
     tokens = queries.shape[0]
     blocks_dev, _, slots, width = prefix.shape[2:]
     wide = queries.shape[1] // (fresh.shape[-1] // width)
@@ -213,16 +213,18 @@
                 pl.BlockSpec((1, 1, 1, 1, slots, width), block_map(kv, j))
                 for kv in (0, 1)
                 for j in range(PATH)
-            ],
+            ]
+            + [pl.BlockSpec(memory_space=pl.ANY)] * len(into),
             out_specs=pl.BlockSpec((tokens, wide), lambda k, chosen, limits, where: (0, where[1] + k)),
         ),
+        input_output_aliases={6 + 2 * PATH: 0} if into else {},
         cost_estimate=pl.CostEstimate(
             flops=8 * count * tokens * wide * keys,
             bytes_accessed=count * 4 * (tokens * wide + keys * width),
             transcendentals=count * tokens * wide // width * keys,
         ),
         compiler_params=pltpu.CompilerParams(vmem_limit_bytes=48 << 20),
-    )(chosen, limits, where, queries, fresh, fresh, *([prefix] * (2 * PATH)))
+    )(chosen, limits, where, queries, fresh, fresh, *([prefix] * (2 * PATH)), *into)
 
 
 def place_kernel(where, piece_ref, whole_ref, out_ref):
@@ -267,11 +269,11 @@
     parts = lax.axis_size("head")
     fresh = fresh_key_value.reshape(2, requests, length, local_kv * head_size)
 
-    def attend_request(query_rows, gathered, low, request, first, count, base, out_heads):
+    def attend_request(query_rows, gathered, low, request, first, count, base, out_heads, into=()):
         pick = functools.partial(lax.dynamic_index_in_dim, axis=0, keepdims=False)
         where = jnp.stack([jnp.int32(request), jnp.int32(base)])
         return attention(
-            query_rows, fresh, gathered, pick(chosen, request), pick(limits, request), where, first, count, out_heads, low
+            query_rows, fresh, gathered, pick(chosen, request), pick(limits, request), where, first, count, out_heads, low, into
         )
 
     def flat_queries(source, request):
@@ -290,7 +292,7 @@
     mine = lax.axis_index("head")
     other = 1 - mine
     theirs = flat_queries(queries, other)
-    half = max(local_kv // 2, 1)
+    half = max(local_kv - 1, 1)
     arrived, held, source, prefix = [], [], queries, prefix_kv
     for low in range(0, local_kv, half):
         high = min(low + half, local_kv)
@@ -310,8 +312,9 @@
         own_rows, gathered, low, mine, low, high - low, mine * local_kv, parts * local_kv
     )
     for low, high, gathered in held[1:]:
-        piece = attend_request(own_rows, gathered, low, mine, low, high - low, 0, high - low)
-        whole = place(whole, piece, jnp.stack([mine * local_kv + low]), wide)
+        whole = attend_request(
+            own_rows, gathered, low, mine, low, high - low, mine * local_kv + low, parts * local_kv, (whole,)
+        )
     for start, piece in arrived:
         whole = place(whole, piece, jnp.stack([other * local_kv + start]), wide)
     return whole

time: 125 us -> 122 us (0.976)
  local copies, waits for them, and re-layouts: 8.07 us -> 13.2 us
  Pallas kernels: 107 us -> 102 us
  starting transfers between devices: 3.27 us -> 1.57 us
    pallas_call x5 -> x4, Pallas kernels: 35.9 us -> 32 us  [attention(): pl.pallas_call(attend, out_shape=jax.ShapeDtypeStruct((tokens, out_heads...]
    unnamed x6 -> x10, local copies, waits for them, and re-layouts: 2.95 us -> 6.51 us
    pallas_call x4 -> x2, Pallas kernels: 7.84 us -> 5.23 us  [place(): pl.pallas_call(place_kernel, out_shape=jax.ShapeDtypeStruct(whole.shape,...]
    ppermute x3 -> x2, starting transfers between devices: 3.27 us -> 1.57 us  [per_device(): arrived.append((start, lax.ppermute(piece, 'head', [(0, 1), (1, 0)])))]
    dynamic_slice x2, local copies, waits for them, and re-layouts: 2.32 us -> 3.91 us  [flat_queries(): rows = lax.dynamic_index_in_dim(source, request, axis=0, keepdims=False)]
  transfers between devices with their start and end apart: 3 -> 2, of which waited for: 1 -> 0; matrix products, arithmetic and copies ran while one was open for 1% -> 3% of each run, Pallas kernels for 51% -> 36%
where the time goes in v6:
time: 122 us; the launch traced here: 121 us
  Pallas kernels  102 us (84%)
  local copies, waits for them, and re-layouts  13.2 us (11%)
  other arithmetic  4.29 us (4%)
  starting transfers between devices  1.57 us (1%)
    pallas_call x2, Pallas kernels, gather(): pl.pallas_call(functools.partial(gather_kernel, columns, low, high), out_...  64.7 us
    pallas_call x4, Pallas kernels, attention(): pl.pallas_call(attend, out_shape=jax.ShapeDtypeStruct((tokens, out_heads...  32 us
    unnamed x10, local copies, waits for them, and re-layouts  6.51 us
    pallas_call x2, Pallas kernels, place(): pl.pallas_call(place_kernel, out_shape=jax.ShapeDtypeStruct(whole.shape,...  5.23 us
    dynamic_slice x2, local copies, waits for them, and re-layouts, flat_queries(): rows = lax.dynamic_index_in_dim(source, request, axis=0, keepdims=False)  3.91 us
    reduce_max x6, other arithmetic, per_device(): best = jnp.max(ranking, axis=1)  3.09 us
  transfers between devices with their start and end apart: 2, of which 0 were waited for; matrix products, arithmetic and copies ran while one was open for 3% of the time, Pallas kernels for 36%

profile of v6, /device:TPU:0, one launch (start us, length us, event | category | flops | bytes accessed | tf_op | source)
XLA Modules:
  0.0 121.2 jit_solution(5869955845800700037)
XLA Ops:
  0.0 0.8 fusion.17
  0.8 0.9 fusion.5
  1.7 0.9 fusion.26
  2.6 0.2 fusion.6
  2.8 0.2 fusion.24
  2.9 0.2 select_reduce_fusion.5
  3.2 0.9 fusion
  4.2 0.1 copy.16
  4.3 0.1 copy.17
  4.4 0.1 copy.18
  4.5 0.1 copy.19
  4.6 0.1 copy.15
  5.3 0.1 stack.24
  5.4 0.1 stack.23
  5.5 1.5 %reshape.205.fk_ref.fv_ref = bf16[2,2,256,512]{3,2,1,0:T(8,128)(2,1)S(1)} reshape(bf16[2,2,256,4,128]{4,3,2,1,0:T(4,128)(2,1)} %param.6) | data formatting | bytes 2097152 | tf_op jit(solution)/shard_map/reshape | solution.py:270
  7.0 2.0 %constant_dynamic-slice_fusion.3 = bf16[1,256,32,128]{3,2,1,0:T(8,128)(2,1)S(1)} fusion(bf16[2,256,32,128]{3,2,1,0:T(8,128)(2,1)} %param.5, s32[]{:T(128)S(6)} %select_n.236), kind=kLoop, calls=%fused_computation.7 | loop fusion | bytes 4194308 | tf_op jit(solution)/shard_map/jit(dynamic_index_in_dim)/dynamic_slice | solution.py:280
  8.9 1.0 copy.26
  9.9 45.2 %shard_map.55.rest_0_.rest_1_.rest_2_.rest_3_.rest_4_.rest_5_.rest_6_.rest_7_.rest_8_.rest_9_.rest_10_.rest_11_ = bf16[16,2,2,3,128,128]{5,4,3,2,1,0:T(8,128)(2,1)} custom-call(bf16[2,2,4,128,128]{4,3,2,1,0:T(8,128)(2,1)} %src.2), custom_call_target="tpu_custom_call" | custom-call | bytes 50331648 | tf_op jit(solution)/shard_map/pallas_call | solution.py:173
  55.1 11.9 %shard_map.56 = bf16[256,3072]{1,0:T(8,128)(2,1)} custom-call(s32[6]{0:T(128)S(1)} %get-tuple-element.30.chosen, s32[6]{0:T(128)S(1)} %get-tuple-element.28.limits, s32[2]{0:T(128)S(1)} %get-tuple-element.44.where, bf16[256,4096]{1,0:T(8,128)(2,1)S(1)} %bitcast.50, bf16[2,2,256,512]{3,2,1,0:T(8,128)(2,1)S(1)} %reshape.205.fk_ref.fv_ref, ...), custom_call_target="tpu_custom_call" | custom-call | flops 6442450944 | bytes 4718592 | tf_op jit(solution)/shard_map/pallas_call | solution.py:204
  67.0 1.4 %collective-permute-start.1 = (bf16[256,3072]{1,0:T(8,128)(2,1)}, bf16[256,3072]{1,0:T(8,128)(2,1)}, u32[]{:S(2)}, u32[]{:S(2)}) collective-permute-start(bf16[256,3072]{1,0:T(8,128)(2,1)} %shard_map.56), channel_id=1, source_target_pairs={{0,1},{1,0},{2,3},{3,2},{4,5},{5,4},{6,7},{7,6},{8,9},{9,8},{10,11... | collective-permute-start | bytes 4718600 | tf_op jit(solution)/shard_map/ppermute | solution.py:308
  68.3 19.6 %shard_map.57.rest_0_.rest_1_.rest_2_.rest_3_.rest_4_.rest_5_.rest_6_.rest_7_.rest_8_.rest_9_.rest_10_.rest_11_ = bf16[16,2,2,1,128,128]{5,4,3,2,1,0:T(8,128)(2,1)} custom-call(bf16[2,2,4,128,128]{4,3,2,1,0:T(8,128)(2,1)} %src.2), custom_call_target="tpu_custom_call" | custom-call | bytes 16777216 | tf_op jit(solution)/shard_map/pallas_call | solution.py:173
  87.9 1.6 %copy-done = bf16[16,2,2,1,128,128]{5,4,3,2,1,0:T(8,128)(2,1)S(1)} copy-done((bf16[16,2,2,1,128,128]{5,4,3,2,1,0:T(8,128)(2,1)S(1)}, bf16[16,2,2,1,128,128]{5,4,3,2,1,0:T(8,128)(2,1)}, u32[]{:S(2)}) %copy-start) | copy-done | bytes 2097176
  89.5 4.2 %shard_map.58 = bf16[256,1024]{1,0:T(8,128)(2,1)} custom-call(s32[6]{0:T(128)S(1)} %get-tuple-element.30.chosen, s32[6]{0:T(128)S(1)} %get-tuple-element.28.limits, s32[2]{0:T(128)S(1)} %get-tuple-element.44.where, bf16[256,4096]{1,0:T(8,128)(2,1)S(1)} %bitcast.51, bf16[2,2,256,512]{3,2,1,0:T(8,128)(2,1)S(1)} %reshape.205.fk_ref.fv_ref, ...), custom_call_target="tpu_custom_call" | custom-call | flops 2147483648 | bytes 1572864 | tf_op jit(solution)/shard_map/pallas_call | solution.py:204
  93.7 0.2 collective-permute-start
  93.9 2.0 %constant_dynamic-slice_fusion = bf16[1,256,32,128]{3,2,1,0:T(8,128)(2,1)S(1)} fusion(bf16[2,256,32,128]{3,2,1,0:T(8,128)(2,1)} %param.5, s32[]{:T(128)S(6)} %select_n.255), kind=kLoop, calls=%fused_computation.4 | loop fusion | bytes 4194308 | tf_op jit(solution)/shard_map/jit(dynamic_index_in_dim)/dynamic_slice | solution.py:280
  95.9 1.0 copy.25
  97.0 11.6 %shard_map.59.rest_12_ = bf16[256,8192]{1,0:T(8,128)(2,1)} custom-call(s32[6]{0:T(128)S(1)} %get-tuple-element.29.chosen, s32[6]{0:T(128)S(1)} %get-tuple-element.27.limits, s32[2]{0:T(128)S(1)} %pad_add_fusion.2.where, bf16[256,4096]{1,0:T(8,128)(2,1)S(1)} %bitcast.48, bf16[2,2,256,512]{3,2,1,0:T(8,128)(2,1)S(1)} %reshape.205.fk_ref.fv_ref, ...), custom_call_target="tpu_custom_call" | custom-call | flops 6442450944 | bytes 4718592 | tf_op jit(solution)/shard_map/pallas_call | solution.py:204
  108.6 1.3 %copy-done.2 = bf16[32,8,32,128]{3,1,2,0:T(8,128)(2,1)} copy-done((bf16[32,8,32,128]{3,1,2,0:T(8,128)(2,1)}, bf16[32,8,32,128]{3,1,2,0:T(8,128)(2,1)S(1)}, u32[]{:S(2)}) %copy-start.2) | copy-done | bytes 2097176
  110.0 1.6 %copy-done.3 = bf16[32,8,32,128]{3,1,2,0:T(8,128)(2,1)S(1)} copy-done((bf16[32,8,32,128]{3,1,2,0:T(8,128)(2,1)S(1)}, bf16[32,8,32,128]{3,1,2,0:T(8,128)(2,1)}, u32[]{:S(2)}) %copy-start.3) | copy-done | bytes 2097176
  111.6 4.3 %shard_map.60.whole_ref = bf16[256,8192]{1,0:T(8,128)(2,1)} custom-call(s32[6]{0:T(128)S(1)} %get-tuple-element.29.chosen, s32[6]{0:T(128)S(1)} %get-tuple-element.27.limits, s32[2]{0:T(128)S(1)} %pad_add_fusion.1.where, bf16[256,4096]{1,0:T(8,128)(2,1)S(1)} %bitcast.49, ...), custom_call_target="tpu_custom_call", output_to_operand_aliasing={{}: (18, {})} | custom-call | flops 2147483648 | bytes 1572864 | tf_op jit(solution)/shard_map/pallas_call | solution.py:204
  115.9 3.4 %shard_map.61.whole_ref = bf16[256,8192]{1,0:T(8,128)(2,1)} custom-call(s32[1]{0:T(128)} %bitcast.16.where, bf16[256,3072]{1,0:T(8,128)(2,1)} %collective-permute-done.1.piece_ref, bf16[256,8192]{1,0:T(8,128)(2,1)} %shard_map.60.whole_ref), custom_call_target="tpu_custom_call", output_to_operand_aliasing={{}: (2, {})} | custom-call | tf_op jit(solution)/shard_map/pallas_call | solution.py:236
  119.3 1.9 %shard_map.62 = bf16[256,8192]{1,0:T(8,128)(2,1)} custom-call(s32[1]{0:T(128)} %bitcast.where, bf16[256,1024]{1,0:T(8,128)(2,1)} %collective-permute-done.piece_ref, bf16[256,8192]{1,0:T(8,128)(2,1)} %shard_map.61.whole_ref), custom_call_target="tpu_custom_call", output_to_operand_aliasing={{}: (2, {})} | custom-call | tf_op jit(solution)/shard_map/pallas_call | solution.py:236
  (31 shorter events, 1.0 us)
Async XLA Ops:
  67.0 48.9 %collective-permute-start.1 = (bf16[256,3072]{1,0:T(8,128)(2,1)}, bf16[256,3072]{1,0:T(8,128)(2,1)}, u32[]{:S(2)}, u32[]{:S(2)}) collective-permute-start(bf16[256,3072]{1,0:T(8,128)(2,1)} %shard_map.56), channel_id=1, source_target_pairs={{0,1},{1,0},{2,3},{3,2},{4,5},{5,4},{6,7},{7,6},{8,9},{9,8},{10,11... | collective-permute-start | bytes 4718600 | tf_op jit(solution)/shard_map/ppermute | solution.py:308
  87.9 1.6 %copy-start = (bf16[16,2,2,1,128,128]{5,4,3,2,1,0:T(8,128)(2,1)S(1)}, bf16[16,2,2,1,128,128]{5,4,3,2,1,0:T(8,128)(2,1)}, u32[]{:S(2)}) copy-start(bf16[16,2,2,1,128,128]{5,4,3,2,1,0:T(8,128)(2,1)} %shard_map.57.rest_0_.rest_1_.rest_2_.rest_3_.rest_4_.rest_5_.rest_6_.rest_7_.rest_8_.rest_9_.rest_10_.rest_11_) | copy-start | bytes 6291460
  93.7 25.6 %collective-permute-start = (bf16[256,1024]{1,0:T(8,128)(2,1)}, bf16[256,1024]{1,0:T(8,128)(2,1)}, u32[]{:S(2)}, u32[]{:S(2)}) collective-permute-start(bf16[256,1024]{1,0:T(8,128)(2,1)} %shard_map.58), channel_id=1, source_target_pairs={{0,1},{1,0},{2,3},{3,2},{4,5},{5,4},{6,7},{7,6},{8,9},{9,8},{10,11... | collective-permute-start | bytes 1572872 | tf_op jit(solution)/shard_map/ppermute | solution.py:308
  97.0 13.0 %copy-start.1 = (bf16[16,2,2,1,128,128]{5,4,3,2,1,0:T(8,128)(2,1)S(1)}, bf16[16,2,2,1,128,128]{5,4,3,2,1,0:T(8,128)(2,1)}, u32[]{:S(2)}) copy-start(bf16[16,2,2,1,128,128]{5,4,3,2,1,0:T(8,128)(2,1)} %shard_map.57.rest_0_.rest_1_.rest_2_.rest_3_.rest_4_.rest_5_.rest_6_.rest_7_.rest_8_.rest_9_.rest_10_.rest_11_) | copy-start | bytes 6291460
  108.6 1.4 %copy-start.2 = (bf16[32,8,32,128]{3,1,2,0:T(8,128)(2,1)}, bf16[32,8,32,128]{3,1,2,0:T(8,128)(2,1)S(1)}, u32[]{:S(2)}) copy-start(bf16[32,8,32,128]{3,1,2,0:T(8,128)(2,1)S(1)} %copy.25) | copy-start | bytes 6291460
  110.0 1.6 %copy-start.3 = (bf16[32,8,32,128]{3,1,2,0:T(8,128)(2,1)S(1)}, bf16[32,8,32,128]{3,1,2,0:T(8,128)(2,1)}, u32[]{:S(2)}) copy-start(bf16[32,8,32,128]{3,1,2,0:T(8,128)(2,1)} %copy-done.2) | copy-start | bytes 6291460
